TPU v7x, 128 devices: a whole 4x4x4 slice. The times are simulated.
128 devices in a mesh: dp: 64 (over x, y, z), tensor: 2 (over core).
Axes of the slice: x: 4, y: 4, z: 4, core: 2. Of those that a mesh axis runs over, the one named last changes fastest.
Arguments:
- momentum: float32 [64, 768, 2560], P(None, ('dp', 'tensor')), may hold values from -6 to 6
- gradient: bfloat16 [64, 768, 2560], P(None, ('dp', 'tensor'))
- assignment: int32 [64], replicated, may hold values from -1 to 63, as said below
Outputs:
- momentum_new: float32 [64, 768, 2560], P(None, ('dp', 'tensor'))
- update: bfloat16 [64, 768, 2560], P(None, ('dp', 'tensor'))
Inputs may be any that keep to these rules, and one draw needn't show every extreme that they name: `assignment`: entry m is the owner of matrix m along dp, or -1 where matrix m takes no update at this step. No owner holds more than 3 matrices, and some owner holds exactly 3.
All inputs are finite; a program needn't handle non-finite values.
Results may differ from a plain program's by a relative error of at most 0.0017.
The roundings to bfloat16 on the way count: a program that leaves them out, or rounds other values in their place, can miss the bound.
Values may be sent and summed in bfloat16 or wider, within the bound.
A program may use at most 128 MiB of HBM per device.

v0:
```python
import math

import jax
import jax.numpy as jnp
from jax import lax
from jax.sharding import PartitionSpec as P

MOST = 3
ITERS = 2


momentum_rate = 0.95
epsilon_norm = 1e-07
linear_term = 3.4445
cubic_term = -4.775
quintic_term = 2.0315


def owner_tables(assignment):
    matrix_count = assignment.shape[0]
    active = assignment >= 0
    same_owner = (assignment[:, None] == assignment[None, :]) & active[None, :]
    earlier = (
        jnp.arange(matrix_count, dtype=jnp.int32)[None, :]
        < jnp.arange(matrix_count, dtype=jnp.int32)[:, None]
    )
    owner_ranks = jnp.sum((same_owner & earlier).astype(jnp.int32), axis=1)
    capacity = MOST
    return (active, assignment, owner_ranks, capacity)


def newton_schulz(matrix_part):
    for repeat in range(ITERS):
        whole_rows = lax.all_gather(matrix_part, "tensor", axis=1, tiled=True)
        gram_rows = jnp.einsum(
            "kid,kjd->kij", matrix_part, whole_rows, preferred_element_type=jnp.float32
        )
        gram_low = gram_rows.astype(jnp.bfloat16)
        gram_whole = lax.all_gather(gram_low, "tensor", axis=1, tiled=True)
        square = jnp.einsum(
            "kij,kjl->kil", gram_low, gram_whole, preferred_element_type=jnp.float32
        )
        mixer_rows = (cubic_term * gram_rows + quintic_term * square).astype(jnp.bfloat16)
        product = jnp.einsum(
            "kij,kjd->kid", mixer_rows, whole_rows, preferred_element_type=jnp.float32
        )
        matrix_part = (linear_term * matrix_part.astype(jnp.float32) + product).astype(jnp.bfloat16)
    return matrix_part


def orthogonalize(arrived):
    item_count, source_count, row_count, col_count = arrived.shape
    matrix_part = arrived.reshape(item_count, source_count * row_count, col_count)
    squares = jnp.sum(jnp.square(matrix_part.astype(jnp.float32)), axis=(1, 2))
    totals = lax.psum(squares, "tensor")
    matrix_part = (
        matrix_part.astype(jnp.float32) / (jnp.sqrt(totals) + epsilon_norm)[:, None, None]
    ).astype(jnp.bfloat16)
    result = newton_schulz(matrix_part)
    return lax.all_to_all(
        result.reshape(item_count, source_count, row_count, col_count),
        "dp",
        split_axis=1,
        concat_axis=1,
        tiled=True,
    )


def on_device(momentum, gradient, assignment):
    devices_dp = lax.axis_size("dp")
    matrix_count = assignment.shape[0]
    active, owners, owner_ranks, capacity = owner_tables(assignment)
    momentum_new = momentum_rate * momentum + gradient.astype(jnp.float32)
    direction = (gradient.astype(jnp.float32) + momentum_rate * momentum_new).astype(jnp.bfloat16)
    slot_index = jnp.arange(capacity, dtype=jnp.int32)[:, None, None]
    owner_index = jnp.arange(devices_dp, dtype=jnp.int32)[None, :, None]
    slot_hits = (
        active[None, None, :]
        & (owners[None, None, :] == owner_index)
        & (owner_ranks[None, None, :] == slot_index)
    )
    matrix_ids = jnp.arange(matrix_count, dtype=jnp.int32)[None, None, :]
    chosen = jnp.sum(slot_hits.astype(jnp.int32) * matrix_ids, axis=2)
    filled = jnp.any(slot_hits, axis=2)
    outgoing = jnp.where(filled[:, :, None, None], direction[chosen], jnp.zeros((), jnp.bfloat16))
    returned = orthogonalize(
        lax.all_to_all(outgoing, "dp", split_axis=1, concat_axis=1, tiled=True)
    )
    picked = returned[jnp.clip(owner_ranks, 0, capacity - 1), jnp.clip(owners, 0, devices_dp - 1)]
    update_scale = math.sqrt(momentum.shape[2])
    update = jnp.where(
        active[:, None, None], update_scale * picked.astype(jnp.float32), jnp.float32(0.0)
    ).astype(jnp.bfloat16)
    return (momentum_new, update)


def solution(mesh):
    placed = (P(None, ("dp", "tensor"), None), P(None, ("dp", "tensor"), None), P())
    return jax.shard_map(
        on_device,
        mesh=mesh,
        in_specs=placed,
        out_specs=(P(None, ("dp", "tensor"), None), P(None, ("dp", "tensor"), None)),
        check_vma=False,
    )
```

profile of v0, /device:TPU:82, one launch (start us, length us, event | category | flops | bytes accessed | tf_op | source)
XLA Modules:
  0.0 489.4 jit_solution(17650862495541514425)
XLA Ops:
  10.0 8.9 %fusion = (bf16[64,6,2560]{2,1,0:T(8,128)(2,1)S(1)}, f32[64,6,2560]{2,1,0:T(8,128)}) fusion(bf16[64,6,2560]{2,0,1:T(8,128)(2,1)} %param.4, f32[64,6,2560]{2,0,1:T(8,128)} %param.3), kind=kLoop, calls=%fused_computation.9 | loop fusion | flops 5898240 | bytes 11796480 | tf_op jit(solution)/shard_map/convert_element_type | solution.py:74
  18.9 8.8 %gather_fusion = bf16[192,6,2560]{2,1,0:T(8,128)(2,1)} fusion(bf16[64,6,2560]{2,1,0:T(8,128)(2,1)S(1)} %get-tuple-element.8, s32[1024]{0:T(1024)S(1)} %pad_clamp_fusion), kind=kCustom, calls=%fused_computation | custom fusion | bytes 11797248 | tf_op jit(solution)/shard_map/gather | solution.py:85
  27.7 4.0 copy_select_fusion
  31.7 97.2 %all_to_all.10 = bf16[3,64,6,2560]{3,2,0,1:T(8,128)(2,1)S(1)} all-to-all(bf16[3,64,6,2560]{3,2,0,1:T(8,128)(2,1)S(1)} %copy_select_fusion), channel_id=1, replica_groups=mesh['dp'=64,'tensor'=2] {'dp'}, dimensions={1} | all-to-all | bytes 11796480 | tf_op jit(solution)/shard_map/all_to_all | solution.py:87
  128.8 3.1 copy-done
  132.0 2.8 multiply_reduce_fusion
  137.4 10.9 %copy.22 = f32[3,64,6,2560]{3,2,1,0:T(8,128)} copy(bf16[3,64,6,2560]{3,2,0,1:T(8,128)(2,1)} %copy-done) | data formatting | bytes 17694720 | tf_op jit(solution)/shard_map/convert_element_type | solution.py:57
  148.3 14.0 %reshape.114 = f32[3,384,2560]{2,1,0:T(8,128)} reshape(f32[3,64,6,2560]{3,2,1,0:T(8,128)} %copy.22) | data formatting | bytes 23592960 | tf_op jit(solution)/shard_map/convert_element_type | solution.py:57
  162.2 8.5 %divide_convert_fusion = bf16[3,384,2560]{2,1,0:T(8,128)(2,1)} fusion(f32[3,384,2560]{2,1,0:T(8,128)} %reshape.114, f32[3]{0:T(128)S(1)} %sqrt_add_fusion), kind=kLoop, calls=%fused_computation.5 | loop fusion | flops 5898240 | bytes 17694732 | tf_op jit(solution)/shard_map/convert_element_type | solution.py:58
  170.8 29.1 %all-gather.5.cloned.1.call-done = bf16[3,768,2560]{2,1,0:T(8,128)(2,1)} async-done(((bf16[3,384,2560]{2,1,0:T(8,128)(2,1)}), bf16[3,768,2560]{2,1,0:T(8,128)(2,1)}) %all-gather.5.cloned.1.call-update) | async-done | bytes 11796496 | tf_op jit(solution)/shard_map/all_gather | solution.py:34
  199.8 13.2 %fusion.19 = (bf16[3,384,768]{2,1,0:T(8,128)(2,1)}, f32[3,384,768]{2,1,0:T(8,128)}) fusion(bf16[3,384,2560]{2,1,0:T(8,128)(2,1)} %divide_convert_fusion, bf16[3,768,2560]{2,1,0:T(8,128)(2,1)} %all-gather.5.cloned.1.call-done), kind=kOutput, calls=%fused_computation.44 | convolution fusion | flops 4530733056 | bytes 23003136 | tf_op jit(solution)/shard_map/kid,kjd->kij/dot_general | solution.py:35
  213.1 16.9 %all-gather.7.cloned.1.call-done = bf16[3,768,768]{2,1,0:T(8,128)(2,1)} async-done(((bf16[3,384,768]{2,1,0:T(8,128)(2,1)}), bf16[3,768,768]{2,1,0:T(8,128)(2,1)}) %all-gather.7.cloned.1.call-update) | async-done | bytes 3538960 | tf_op jit(solution)/shard_map/all_gather | solution.py:39
  230.0 17.4 %add_convert_fusion.1 = bf16[3,384,2560]{2,1,0:T(8,128)(2,1)} fusion(bf16[3,384,2560]{2,1,0:T(8,128)(2,1)} %divide_convert_fusion, bf16[3,768,2560]{2,1,0:T(8,128)(2,1)} %all-gather.5.cloned.1.call-done, f32[3,384,768]{2,1,0:T(8,128)} %get-tuple-element.11, bf16[3,384,768]{2,1,0:T(8,128)(2,1)} %get-tuple-element.10, ...), kind=kOutput, calls=%fused_computation.4 | convolution fusion | flops 5904138240 | bytes 32440320 | tf_op jit(solution)/shard_map/kij,kjd->kid/dot_general | solution.py:44
  247.7 27.8 %all-gather.9.cloned.1.call-done = bf16[3,768,2560]{2,1,0:T(8,128)(2,1)} async-done(((bf16[3,384,2560]{2,1,0:T(8,128)(2,1)}), bf16[3,768,2560]{2,1,0:T(8,128)(2,1)}) %all-gather.9.cloned.1.call-update) | async-done | bytes 11796496 | tf_op jit(solution)/shard_map/all_gather | solution.py:34
  275.4 13.2 %fusion.20 = (bf16[3,384,768]{2,1,0:T(8,128)(2,1)}, f32[3,384,768]{2,1,0:T(8,128)}) fusion(bf16[3,384,2560]{2,1,0:T(8,128)(2,1)} %add_convert_fusion.1, bf16[3,768,2560]{2,1,0:T(8,128)(2,1)} %all-gather.9.cloned.1.call-done), kind=kOutput, calls=%fused_computation.45 | convolution fusion | flops 4530733056 | bytes 23003136 | tf_op jit(solution)/shard_map/kid,kjd->kij/dot_general | solution.py:35
  288.6 16.9 %all-gather.11.cloned.1.call-done = bf16[3,768,768]{2,1,0:T(8,128)(2,1)} async-done(((bf16[3,384,768]{2,1,0:T(8,128)(2,1)}), bf16[3,768,768]{2,1,0:T(8,128)(2,1)}) %all-gather.11.cloned.1.call-update) | async-done | bytes 3538960 | tf_op jit(solution)/shard_map/all_gather | solution.py:39
  305.5 17.4 %add_convert_fusion = bf16[3,384,2560]{2,1,0:T(8,128)(2,1)} fusion(bf16[3,384,2560]{2,1,0:T(8,128)(2,1)} %add_convert_fusion.1, bf16[3,768,2560]{2,1,0:T(8,128)(2,1)} %all-gather.9.cloned.1.call-done, f32[3,384,768]{2,1,0:T(8,128)} %get-tuple-element.13, bf16[3,384,768]{2,1,0:T(8,128)(2,1)} %get-tuple-element.12, ...), kind=kOutput, calls=%fused_computation.3 | convolution fusion | flops 5904138240 | bytes 32440320 | tf_op jit(solution)/shard_map/kij,kjd->kid/dot_general | solution.py:44
  322.9 10.1 %reshape.113 = bf16[3,64,6,2560]{3,2,1,0:T(8,128)(2,1)} reshape(bf16[3,384,2560]{2,1,0:T(8,128)(2,1)} %add_convert_fusion) | data formatting | bytes 11796480 | tf_op jit(solution)/shard_map/reshape | solution.py:61
  333.1 6.8 %copy.23 = bf16[3,64,6,2560]{3,2,0,1:T(8,128)(2,1)} copy(bf16[3,64,6,2560]{3,2,1,0:T(8,128)(2,1)} %reshape.113) | data formatting | bytes 11796480 | tf_op jit(solution)/shard_map/reshape | solution.py:61
  339.8 10.4 %all-to-all-start.1 = ((bf16[3,64,6,2560]{3,2,0,1:T(8,128)(2,1)}), bf16[3,64,6,2560]{3,2,0,1:T(8,128)(2,1)}, u32[]{:S(2)}, u32[]{:S(2)}) async-start(bf16[3,64,6,2560]{3,2,0,1:T(8,128)(2,1)} %copy.23), calls=%async_computation.1 | async-start | bytes 15728640 | tf_op jit(solution)/shard_map/all_to_all | solution.py:60
  350.3 6.7 %copy.25 = f32[64,6,2560]{2,0,1:T(8,128)} copy(f32[64,6,2560]{2,1,0:T(8,128)} %get-tuple-element.9) | data formatting | bytes 7864320
  357.0 112.3 %all-to-all-done.1 = bf16[3,64,6,2560]{3,2,0,1:T(8,128)(2,1)} async-done(((bf16[3,64,6,2560]{3,2,0,1:T(8,128)(2,1)}), bf16[3,64,6,2560]{3,2,0,1:T(8,128)(2,1)}, u32[]{:S(2)}, u32[]{:S(2)}) %all-to-all-start.1) | async-done | bytes 5898272 | tf_op jit(solution)/shard_map/all_to_all | solution.py:60
  469.3 7.1 %copy.24 = bf16[3,64,6,2560]{3,2,1,0:T(8,128)(2,1)} copy(bf16[3,64,6,2560]{3,2,0,1:T(8,128)(2,1)} %all-to-all-done.1) | data formatting | bytes 11796480 | tf_op jit(solution)/shard_map/all_to_all | solution.py:60
  476.4 3.9 gather_fusion.1
  (26 shorter events, 8.4 us)
Async XLA Ops:
  7.2 192.7 %all-gather.5.cloned.1.call-start = ((), (), s32[]{:S(2)}) async-start(), calls=%async_computation.2 | async-start | bytes 17694720 | tf_op jit(solution)/shard_map/all_gather | solution.py:34
  128.8 3.1 copy-start
  170.7 59.2 %all-gather.7.cloned.1.call-start = ((), (), s32[]{:S(2)}) async-start(), calls=%async_computation.3 | async-start | bytes 5308416 | tf_op jit(solution)/shard_map/all_gather | solution.py:39
  213.0 62.4 %all-gather.9.cloned.1.call-start = ((), (), s32[]{:S(2)}) async-start(), calls=%async_computation.4 | async-start | bytes 17694720 | tf_op jit(solution)/shard_map/all_gather | solution.py:34
  247.4 58.1 %all-gather.11.cloned.1.call-start = ((), (), s32[]{:S(2)}) async-start(), calls=%async_computation.5 | async-start | bytes 5308416 | tf_op jit(solution)/shard_map/all_gather | solution.py:39
  339.8 129.5 %all-to-all-start.1 = ((bf16[3,64,6,2560]{3,2,0,1:T(8,128)(2,1)}), bf16[3,64,6,2560]{3,2,0,1:T(8,128)(2,1)}, u32[]{:S(2)}, u32[]{:S(2)}) async-start(bf16[3,64,6,2560]{3,2,0,1:T(8,128)(2,1)} %copy.23), calls=%async_computation.1 | async-start | bytes 15728640 | tf_op jit(solution)/shard_map/all_to_all | solution.py:60
  350.2 6.7 %copy-start.1 = (s32[64]{0:T(128)S(1)}, s32[64]{0:T(128)}, u32[]{:S(2)}) copy-start(s32[64]{0:T(128)} %param.5) | copy-start | bytes 772
Sparse Core Ops, SparseCore 0:
  170.8 28.9 all-gather.4
  213.2 16.7 all-gather.6
  247.5 27.8 all-gather.8
  288.8 16.7 all-gather.10
where the time goes:
time: 490 us; the launch traced here: 489 us
  waiting for transfers between devices  203 us (41%)
  blocking collectives  99.8 us (20%)
  local copies, waits for them, and re-layouts  73.5 us (15%)
  matrix products  61.2 us (12%)
  other arithmetic  27.4 us (6%)
  between operations  13.8 us (3%)
  starting transfers between devices  10.8 us (2%)
    all_to_all x1, waiting for transfers between devices, orthogonalize(): lax.all_to_all(result.reshape(item_count, source_count, row_count, col_co...  112 us
    all_to_all x1, blocking collectives, on_device(): lax.all_to_all(outgoing, 'dp', split_axis=1, concat_axis=1, tiled=True)  97.2 us
    all_gather x2, waiting for transfers between devices, newton_schulz(): whole_rows = lax.all_gather(matrix_part, 'tensor', axis=1, tiled=True)  56.8 us
    dot_general x2, matrix products, newton_schulz(): jnp.einsum('kij,kjd->kid', mixer_rows, whole_rows, preferred_element_type...  34.8 us
    all_gather x2, waiting for transfers between devices, newton_schulz(): gram_whole = lax.all_gather(gram_low, 'tensor', axis=1, tiled=True)  33.7 us
    dot_general x2, matrix products, newton_schulz(): jnp.einsum('kid,kjd->kij', matrix_part, whole_rows, preferred_element_typ...  26.4 us
    convert_element_type x2, local copies, waits for them, and re-layouts, orthogonalize(): matrix_part.astype(jnp.float32)  24.8 us
    reshape x2, local copies, waits for them, and re-layouts, orthogonalize(): result.reshape(item_count, source_count, row_count, col_count)  16.9 us
  transfers between devices with their start and end apart: 5, of which 5 were waited for; matrix products, arithmetic and copies ran while one was open for 1% of the time, Pallas kernels for 0%

commit v1 on v0

--- a/solution.py
+++ b/solution.py
@@ -5,7 +5,6 @@
 from jax import lax
 from jax.sharding import PartitionSpec as P
 
-MOST = 3
 ITERS = 2
 
 
@@ -14,19 +13,6 @@
 linear_term = 3.4445
 cubic_term = -4.775
 quintic_term = 2.0315
-
-
-def owner_tables(assignment):
-    matrix_count = assignment.shape[0]
-    active = assignment >= 0
-    same_owner = (assignment[:, None] == assignment[None, :]) & active[None, :]
-    earlier = (
-        jnp.arange(matrix_count, dtype=jnp.int32)[None, :]
-        < jnp.arange(matrix_count, dtype=jnp.int32)[:, None]
-    )
-    owner_ranks = jnp.sum((same_owner & earlier).astype(jnp.int32), axis=1)
-    capacity = MOST
-    return (active, assignment, owner_ranks, capacity)
 
 
 def newton_schulz(matrix_part):
@@ -67,29 +53,14 @@
 
 
 def on_device(momentum, gradient, assignment):
-    devices_dp = lax.axis_size("dp")
-    matrix_count = assignment.shape[0]
-    active, owners, owner_ranks, capacity = owner_tables(assignment)
-    momentum_new = momentum_rate * momentum + gradient.astype(jnp.float32)
-    direction = (gradient.astype(jnp.float32) + momentum_rate * momentum_new).astype(jnp.bfloat16)
-    slot_index = jnp.arange(capacity, dtype=jnp.int32)[:, None, None]
-    owner_index = jnp.arange(devices_dp, dtype=jnp.int32)[None, :, None]
-    slot_hits = (
-        active[None, None, :]
-        & (owners[None, None, :] == owner_index)
-        & (owner_ranks[None, None, :] == slot_index)
-    )
-    matrix_ids = jnp.arange(matrix_count, dtype=jnp.int32)[None, None, :]
-    chosen = jnp.sum(slot_hits.astype(jnp.int32) * matrix_ids, axis=2)
-    filled = jnp.any(slot_hits, axis=2)
-    outgoing = jnp.where(filled[:, :, None, None], direction[chosen], jnp.zeros((), jnp.bfloat16))
-    returned = orthogonalize(
-        lax.all_to_all(outgoing, "dp", split_axis=1, concat_axis=1, tiled=True)
-    )
-    picked = returned[jnp.clip(owner_ranks, 0, capacity - 1), jnp.clip(owners, 0, devices_dp - 1)]
+    wide = gradient.astype(jnp.float32)
+    momentum_new = momentum_rate * momentum + wide
+    direction = (wide + momentum_rate * momentum_new).astype(jnp.bfloat16)
+    arrived = lax.all_to_all(direction, "dp", split_axis=0, concat_axis=0, tiled=True)
+    returned = orthogonalize(arrived[None])[0]
     update_scale = math.sqrt(momentum.shape[2])
     update = jnp.where(
-        active[:, None, None], update_scale * picked.astype(jnp.float32), jnp.float32(0.0)
+        (assignment >= 0)[:, None, None], update_scale * returned.astype(jnp.float32), jnp.float32(0.0)
     ).astype(jnp.bfloat16)
     return (momentum_new, update)
 

time: 490 us -> 213 us (0.43)
  the two profiles are of different devices: /device:TPU:82 before, /device:TPU:1 now
where the time goes in v1:
time: 213 us; the launch traced here: 212 us
  waiting for transfers between devices  81.3 us (38%)
  blocking collectives  51 us (24%)
  matrix products  22.8 us (11%)
  local copies, waits for them, and re-layouts  18.3 us (9%)
  between operations  14.5 us (7%)
  other arithmetic  13.7 us (6%)
  starting transfers between devices  10.5 us (5%)
    all_to_all x1, blocking collectives, on_device(): lax.all_to_all(direction, 'dp', split_axis=0, concat_axis=0, tiled=True)  45.7 us
    all_gather x2, waiting for transfers between devices, newton_schulz(): whole_rows = lax.all_gather(matrix_part, 'tensor', axis=1, tiled=True)  27.2 us
    all_to_all x1, waiting for transfers between devices, orthogonalize(): lax.all_to_all(result.reshape(item_count, source_count, row_count, col_co...  27.2 us
    all_gather x2, waiting for transfers between devices, newton_schulz(): gram_whole = lax.all_gather(gram_low, 'tensor', axis=1, tiled=True)  26.8 us
    dot_general x2, matrix products, newton_schulz(): jnp.einsum('kij,kjd->kid', mixer_rows, whole_rows, preferred_element_type...  12.3 us
    dot_general x2, matrix products, newton_schulz(): jnp.einsum('kid,kjd->kij', matrix_part, whole_rows, preferred_element_typ...  10.5 us
    all_to_all x1, starting transfers between devices, orthogonalize(): lax.all_to_all(result.reshape(item_count, source_count, row_count, col_co...  10.1 us
    unnamed x10, local copies, waits for them, and re-layouts  10 us
  transfers between devices with their start and end apart: 5, of which 5 were waited for; matrix products, arithmetic and copies ran while one was open for 4% of the time, Pallas kernels for 0%

profile of v1, /device:TPU:1, one launch (start us, length us, event | category | flops | bytes accessed | tf_op | source)
XLA Modules:
  0.0 212.0 jit_solution(16570477342495389945)
XLA Ops:
  7.2 8.9 %fusion = (bf16[64,6,2560]{2,1,0:T(8,128)(2,1)S(1)}, f32[64,6,2560]{2,1,0:T(8,128)}) fusion(bf16[64,6,2560]{2,0,1:T(8,128)(2,1)} %param.4, f32[64,6,2560]{2,0,1:T(8,128)} %param.3), kind=kLoop, calls=%fused_computation.4 | loop fusion | flops 5898240 | bytes 11796480 | tf_op jit(solution)/shard_map/convert_element_type | solution.py:58
  16.1 45.7 %all_to_all.10 = bf16[64,6,2560]{2,1,0:T(8,128)(2,1)S(1)} all-to-all(bf16[64,6,2560]{2,1,0:T(8,128)(2,1)S(1)} %get-tuple-element.6), channel_id=1, replica_groups=mesh['dp'=64,'tensor'=2] {'dp'}, dimensions={0} | all-to-all | bytes 3932160 | tf_op jit(solution)/shard_map/all_to_all | solution.py:59
  61.8 1.5 copy-done
  63.3 1.9 fusion.1
  65.3 5.3 %psum.7 = f32[1]{0:T(128)} all-reduce(f32[1]{0:T(128)} %bitcast), channel_id=1, replica_groups=mesh['dp'=64,'tensor'=2] {'tensor'}, use_global_device_ids=true, to_apply=%region_1.0 | all-reduce | flops 1 | bytes 8 | tf_op jit(solution)/shard_map/psum | solution.py:41
  71.2 2.2 %fusion.2 = bf16[64,6,2560]{2,1,0:T(8,128)(2,1)S(1)} fusion(bf16[64,6,2560]{2,1,0:T(8,128)(2,1)} %copy-done, f32[]{:T(128)} %bitcast.1), kind=kLoop, calls=%fused_computation.6 | loop fusion | flops 2949120 | bytes 3932164 | tf_op jit(solution)/shard_map/convert_element_type | solution.py:44
  73.4 2.1 convert_element_type.95
  75.5 0.0 all-gather.10.cloned.1.call-start
  75.6 2.1 convert_element_type.93
  77.6 10.0 %all-gather.8.cloned.1.call-done = bf16[1,768,2560]{2,1,0:T(8,128)(2,1)} async-done(((bf16[1,384,2560]{2,1,0:T(8,128)(2,1)}), bf16[1,768,2560]{2,1,0:T(8,128)(2,1)}) %all-gather.8.cloned.1.call-update) | async-done | bytes 3932176 | tf_op jit(solution)/shard_map/all_gather | solution.py:20
  87.6 5.3 %fusion.21 = (bf16[384,768]{1,0:T(8,128)(2,1)}, f32[384,768]{1,0:T(8,128)S(1)}) fusion(bf16[384,2560]{1,0:T(8,128)(2,1)} %convert_element_type.93, bf16[1,768,2560]{2,1,0:T(8,128)(2,1)} %all-gather.8.cloned.1.call-done), kind=kOutput, calls=%fused_computation.32 | convolution fusion | flops 1510244352 | bytes 7667712 | tf_op jit(solution)/shard_map/kid,kjd->kij/dot_general | solution.py:21
  93.0 13.4 %all-gather.10.cloned.1.call-done = bf16[768,768]{1,0:T(8,128)(2,1)} async-done(((bf16[384,768]{1,0:T(8,128)(2,1)}), bf16[768,768]{1,0:T(8,128)(2,1)}) %all-gather.10.cloned.1.call-update) | async-done | bytes 1179664 | tf_op jit(solution)/shard_map/all_gather | solution.py:25
  106.3 6.1 %fusion.4 = bf16[384,2560]{1,0:T(8,128)(2,1)} fusion(bf16[1,768,2560]{2,1,0:T(8,128)(2,1)} %all-gather.8.cloned.1.call-done, bf16[384,2560]{1,0:T(8,128)(2,1)S(1)} %copy-done.2, bf16[384,768]{1,0:T(8,128)(2,1)} %get-tuple-element.8, bf16[768,768]{1,0:T(8,128)(2,1)} %all-gather.10.cloned.1.call-done, f32[384,768]{1,0:T(8,128)S(1)} %get-tuple-element.9), kind=kOutput, calls=%fused_computation.12 | convolution fusion | flops 1968046080 | bytes 10813440 | tf_op jit(solution)/shard_map/kij,kjd->kid/dot_general | solution.py:30
  112.5 0.2 all-gather.14.cloned.1.call-start
  112.7 17.2 %all-gather.12.cloned.1.call-done = bf16[768,2560]{1,0:T(8,128)(2,1)} async-done(((bf16[384,2560]{1,0:T(8,128)(2,1)}), bf16[768,2560]{1,0:T(8,128)(2,1)}) %all-gather.12.cloned.1.call-update) | async-done | bytes 3932176 | tf_op jit(solution)/shard_map/all_gather | solution.py:20
  130.0 5.2 %fusion.22 = (bf16[384,768]{1,0:T(8,128)(2,1)}, f32[384,768]{1,0:T(8,128)S(1)}) fusion(bf16[384,2560]{1,0:T(8,128)(2,1)} %fusion.4, bf16[768,2560]{1,0:T(8,128)(2,1)} %all-gather.12.cloned.1.call-done), kind=kOutput, calls=%fused_computation.33 | convolution fusion | flops 1510244352 | bytes 7667712 | tf_op jit(solution)/shard_map/kid,kjd->kij/dot_general | solution.py:21
  135.2 13.4 %all-gather.14.cloned.1.call-done = bf16[768,768]{1,0:T(8,128)(2,1)} async-done(((bf16[384,768]{1,0:T(8,128)(2,1)}), bf16[768,768]{1,0:T(8,128)(2,1)}) %all-gather.14.cloned.1.call-update) | async-done | bytes 1179664 | tf_op jit(solution)/shard_map/all_gather | solution.py:25
  148.7 6.1 %fusion.5 = bf16[384,2560]{1,0:T(8,128)(2,1)} fusion(bf16[768,2560]{1,0:T(8,128)(2,1)} %all-gather.12.cloned.1.call-done, bf16[384,2560]{1,0:T(8,128)(2,1)S(1)} %copy-done.1, bf16[384,768]{1,0:T(8,128)(2,1)} %get-tuple-element.10, bf16[768,768]{1,0:T(8,128)(2,1)} %all-gather.14.cloned.1.call-done, f32[384,768]{1,0:T(8,128)S(1)} %get-tuple-element.11), kind=kOutput, calls=%fused_computation.13 | convolution fusion | flops 1968046080 | bytes 10813440 | tf_op jit(solution)/shard_map/kij,kjd->kid/dot_general | solution.py:30
  154.8 4.1 %reshape.103 = bf16[1,64,6,2560]{3,2,1,0:T(8,128)(2,1)} reshape(bf16[384,2560]{1,0:T(8,128)(2,1)} %fusion.5) | data formatting | bytes 3932160 | tf_op jit(solution)/shard_map/reshape | solution.py:47
  158.9 10.1 %all-to-all-start.1 = ((bf16[1,64,6,2560]{3,2,0,1:T(8,128)(2,1)}), bf16[1,64,6,2560]{3,2,0,1:T(8,128)(2,1)S(1)}, u32[]{:S(2)}, u32[]{:S(2)}) async-start(bf16[1,64,6,2560]{3,2,0,1:T(8,128)(2,1)} %bitcast.22), calls=%async_computation.1 | async-start | bytes 5242880 | tf_op jit(solution)/shard_map/all_to_all | solution.py:46
  169.1 6.7 %copy.13 = f32[64,6,2560]{2,0,1:T(8,128)} copy(f32[64,6,2560]{2,1,0:T(8,128)} %get-tuple-element.7) | data formatting | bytes 7864320
  175.8 27.2 %all-to-all-done.1 = bf16[1,64,6,2560]{3,2,0,1:T(8,128)(2,1)S(1)} async-done(((bf16[1,64,6,2560]{3,2,0,1:T(8,128)(2,1)}), bf16[1,64,6,2560]{3,2,0,1:T(8,128)(2,1)S(1)}, u32[]{:S(2)}, u32[]{:S(2)}) %all-to-all-start.1) | async-done | bytes 1966112 | tf_op jit(solution)/shard_map/all_to_all | solution.py:46
  202.9 0.7 fusion.3
  203.6 1.8 copy.14
  (14 shorter events, 0.2 us)
Async XLA Ops:
  7.2 80.5 %all-gather.8.cloned.1.call-start = ((), (), s32[]{:S(2)}) async-start(), calls=%async_computation.2 | async-start | bytes 5898240 | tf_op jit(solution)/shard_map/all_gather | solution.py:20
  61.8 1.5 copy-start
  75.5 30.8 %all-gather.10.cloned.1.call-start = ((), (), s32[]{:S(2)}) async-start(), calls=%async_computation.3 | async-start | bytes 1769472 | tf_op jit(solution)/shard_map/all_gather | solution.py:25
  77.6 28.7 %copy-start.2 = (bf16[384,2560]{1,0:T(8,128)(2,1)S(1)}, bf16[384,2560]{1,0:T(8,128)(2,1)}, u32[]{:S(2)}) copy-start(bf16[384,2560]{1,0:T(8,128)(2,1)} %convert_element_type.93) | copy-start | bytes 5898244
  92.9 37.1 %all-gather.12.cloned.1.call-start = ((), (), s32[]{:S(2)}) async-start(), calls=%async_computation.4 | async-start | bytes 5898240 | tf_op jit(solution)/shard_map/all_gather | solution.py:20
  112.5 36.2 %copy-start.1 = (bf16[384,2560]{1,0:T(8,128)(2,1)S(1)}, bf16[384,2560]{1,0:T(8,128)(2,1)}, u32[]{:S(2)}) copy-start(bf16[384,2560]{1,0:T(8,128)(2,1)} %fusion.4) | copy-start | bytes 5898244
  112.5 36.2 %all-gather.14.cloned.1.call-start = ((), (), s32[]{:S(2)}) async-start(), calls=%async_computation.5 | async-start | bytes 1769472 | tf_op jit(solution)/shard_map/all_gather | solution.py:25
  158.9 44.0 %all-to-all-start.1 = ((bf16[1,64,6,2560]{3,2,0,1:T(8,128)(2,1)}), bf16[1,64,6,2560]{3,2,0,1:T(8,128)(2,1)S(1)}, u32[]{:S(2)}, u32[]{:S(2)}) async-start(bf16[1,64,6,2560]{3,2,0,1:T(8,128)(2,1)} %bitcast.22), calls=%async_computation.1 | async-start | bytes 5242880 | tf_op jit(solution)/shard_map/all_to_all | solution.py:46
  169.0 6.7 %copy-start.3 = (s32[64]{0:T(128)S(1)}, s32[64]{0:T(128)}, u32[]{:S(2)}) copy-start(s32[64]{0:T(128)} %param.5) | copy-start | bytes 772
Sparse Core Ops, SparseCore 0:
  75.6 11.9 all-gather.7
  93.0 13.2 all-gather.9
  112.6 17.3 all-gather.11
  135.3 13.2 all-gather.13

commit v2 on v1

v2 whole, which is shorter than its diff:
```python
import functools
import math

import jax
import jax.numpy as jnp
from jax import lax
from jax.experimental import pallas as pl
from jax.experimental.pallas import tpu as pltpu
from jax.sharding import PartitionSpec as P

ITERS = 2
MESH = pl.DeviceIdType.MESH

momentum_rate = 0.95
epsilon_norm = 1e-07
linear_term = 3.4445
cubic_term = -4.775
quintic_term = 2.0315

SIDE = 4
CHIPS = SIDE**3
LOCAL = 6
WIDTH = 2560
LANES = 128
TILES = WIDTH // LANES
ROWS = LOCAL * CHIPS * 2
HALF = LOCAL * CHIPS
LINES = LOCAL * TILES
BLOCK = (8, LINES // 8 * LANES)
PITCH = LINES + 1
GROUP = 16
GROUPS = CHIPS // GROUP
HALVES = 2
SLOTS = CHIPS // HALVES
STEP = 512
TILE = 256
STRIPS = ROWS // TILE
STRIDE = 27


def position():
    return lax.axis_index("dp"), lax.axis_index("tensor")


def moved(index, sign):
    place, _ = position()
    offset = index * STRIDE % CHIPS
    spot = 0
    for scale in (SIDE * SIDE, SIDE, 1):
        here = place // scale % SIDE
        away = offset // scale % SIDE
        spot = spot + (here + sign * away + SIDE) % SIDE * scale
    return spot


def line_of(row, tile):
    return tile * LOCAL + row


def write_lines(scratch, row, tile, values):
    scratch[pl.ds(line_of(row, tile), 8, stride=PITCH), :] = values


def read_lines(scratch, row, tile):
    return scratch[pl.ds(line_of(row, tile), 8, stride=PITCH), :]


def pack_eight(scratch, blocks, first):
    for item in range(8):
        for part in range(LINES // 8):
            values = scratch[pl.ds(item * PITCH + 8 * part, 8), :]
            blocks[first + item, :, part * LANES : (part + 1) * LANES] = values.astype(jnp.bfloat16)


def unpack_eight(scratch, blocks, first):
    for item in range(8):
        values = blocks[first + item].astype(jnp.float32)
        for part in range(LINES // 8):
            scratch[pl.ds(item * PITCH + 8 * part, 8), :] = values[:, part * LANES : (part + 1) * LANES]


def product(a, b, dims):
    return lax.dot_general(a, b, (dims, ((), ())), preferred_element_type=jnp.float32)


def strip(index):
    return slice(index * TILE, (index + 1) * TILE)


def gram_of(x_ref, gram, low):
    for i in range(STRIPS):
        for j in range(i + 1):
            value = product(x_ref[strip(i), :], x_ref[strip(j), :], ((1,), (1,)))
            gram[strip(i), strip(j)] = value
            rounded = value.astype(jnp.bfloat16)
            low[strip(i), strip(j)] = rounded
            if i != j:
                low[strip(j), strip(i)] = value.T.astype(jnp.bfloat16)


def mixer_of(gram, low, mixer):
    for j in range(STRIPS):
        for i in range(j, STRIPS):
            square = product(low[strip(i), :], low[:, strip(j)], ((1,), (0,)))
            value = cubic_term * gram[strip(i), strip(j)] + quintic_term * square
            mixer[strip(i), strip(j)] = value.astype(jnp.bfloat16)
            if i != j:
                mixer[strip(j), strip(i)] = value.T.astype(jnp.bfloat16)


def kernel(
    momentum, gradient, assignment, momentum_new, update,
    mom_in, grad_in, sent, arrived, returned, x_now, x_next, gram, low, mixer, lines, squares, squares_in,
    load_sems, out_sem, in_sems, back_out_sem, back_sems, pair_out_sem, pair_sems, square_sems,
):
    place, core = position()
    pair = (place, 1 - core)

    def load(group):
        rows = pl.ds(pl.multiple_of(group * GROUP, GROUP), GROUP)
        return (
            pltpu.make_async_copy(momentum.at[:, rows, :], mom_in.at[group], load_sems.at[0, group]),
            pltpu.make_async_copy(gradient.at[:, rows, :], grad_in.at[group], load_sems.at[1, group]),
        )

    for group in range(GROUPS):
        for copy in load(group):
            copy.start()

    barrier = pltpu.get_barrier_semaphore()
    pl.semaphore_signal(barrier, inc=1, device_id=pair, device_id_type=MESH)

    def greet(index, carry):
        pl.semaphore_signal(barrier, inc=1, device_id=(moved(index, 1), core), device_id_type=MESH)
        return carry

    lax.fori_loop(1, CHIPS, greet, 0)

    def prepare(group, carry):
        for copy in load(group):
            copy.wait()
        rows = pl.ds(pl.multiple_of(group * GROUP, GROUP), GROUP)
        for row in range(LOCAL):
            for tile in range(TILES):
                columns = slice(tile * LANES, (tile + 1) * LANES)
                wide = grad_in[group, row, :, columns].astype(jnp.float32)
                fresh = momentum_rate * mom_in[group, row, :, columns] + wide
                momentum_new[row, rows, columns] = fresh
                direction = wide + momentum_rate * fresh
                for eight in range(2):
                    write_lines(lines.at[eight], row, tile, direction[eight * 8 : eight * 8 + 8])
        for eight in range(2):
            pack_eight(lines.at[eight], sent, group * GROUP + eight * 8)
        return carry

    lax.fori_loop(0, GROUPS, prepare, 0)

    pl.semaphore_wait(barrier, CHIPS)

    pltpu.make_async_copy(sent.at[place], arrived.at[0], in_sems.at[0]).start()

    def send(index, carry):
        target = moved(index, 1)
        pltpu.make_async_remote_copy(
            src_ref=sent.at[target], dst_ref=arrived.at[index], send_sem=out_sem, recv_sem=in_sems.at[index // GROUP],
            device_id=(target, core), device_id_type=MESH,
        ).start()
        return carry

    lax.fori_loop(1, CHIPS, send, 0)

    def rows_of(group, row):
        start = group // (GROUPS // HALVES) * (LOCAL * SLOTS) + row * SLOTS + group % (GROUPS // HALVES) * GROUP
        return pl.multiple_of(start, GROUP)

    def relay(group, row):
        start = rows_of(group, row)
        return pltpu.make_async_remote_copy(
            src_ref=x_now.at[pl.ds(start, GROUP), :], dst_ref=x_now.at[pl.ds(HALF + start, GROUP), :],
            send_sem=pair_out_sem, recv_sem=pair_sems.at[0], device_id=pair, device_id_type=MESH,
        )

    squares[...] = jnp.zeros_like(squares)

    def accept(group, carry):
        span = arrived.at[pl.ds(group * GROUP, GROUP)]
        pltpu.make_async_copy(span, span, in_sems.at[group]).wait()
        for eight in range(2):
            unpack_eight(lines.at[eight], arrived, group * GROUP + eight * 8)
        for row in range(LOCAL):
            start = rows_of(group, row)
            total = jnp.zeros((8, LANES), jnp.float32)
            for tile in range(TILES):
                values = [read_lines(lines.at[eight], row, tile) for eight in range(2)]
                for value in values:
                    total += value * value
                x_now[pl.ds(start, GROUP), tile * LANES : (tile + 1) * LANES] = jnp.concatenate(
                    values, axis=0
                ).astype(jnp.bfloat16)
            squares[...] += total
            relay(group, row).start()
        return carry

    lax.fori_loop(0, GROUPS, accept, 0)

    swap = pltpu.make_async_remote_copy(
        src_ref=squares, dst_ref=squares_in, send_sem=square_sems.at[0], recv_sem=square_sems.at[1],
        device_id=pair, device_id_type=MESH,
    )
    swap.start()
    swap.wait()
    own, other = x_now.at[pl.ds(0, HALF), :], x_now.at[pl.ds(HALF, HALF), :]
    pltpu.make_async_copy(own, own, pair_out_sem).wait()
    pltpu.make_async_copy(other, other, pair_sems.at[0]).wait()

    norm = jnp.sqrt(jnp.sum(squares[...] + squares_in[...])) + epsilon_norm

    def normalize(index, carry):
        rows = pl.ds(pl.multiple_of(index * 32, 32), 32)
        x_now[rows, :] = (x_now[rows, :].astype(jnp.float32) / norm).astype(jnp.bfloat16)
        return carry

    lax.fori_loop(0, ROWS // 32, normalize, 0)

    gram_of(x_now, gram, low)
    mixer_of(gram, low, mixer)

    def mix(index, carry):
        columns = pl.ds(pl.multiple_of(index * STEP, STEP), STEP)
        for i in range(STRIPS):
            value = product(mixer[strip(i), :], x_now[:, columns], ((1,), (0,)))
            x_next[strip(i), columns] = (
                linear_term * x_now[strip(i), columns].astype(jnp.float32) + value
            ).astype(jnp.bfloat16)
        return carry

    lax.fori_loop(0, WIDTH // STEP, mix, 0)

    gram_of(x_next, gram, low)
    mixer_of(gram, low, mixer)

    active = assignment[place] >= 0
    part = LOCAL * SLOTS

    def finish(half, carry):
        rows = pl.ds(pl.multiple_of(half * part, part), part)

        def columns_step(index, inner):
            columns = pl.ds(pl.multiple_of(index * STEP, STEP), STEP)
            value = linear_term * x_next[rows, columns].astype(jnp.float32) + product(
                mixer[rows, :], x_next[:, columns], ((1,), (0,))
            )
            value = math.sqrt(WIDTH) * value.astype(jnp.bfloat16).astype(jnp.float32)
            value = jnp.where(active, value, 0.0)
            for row in range(LOCAL):
                for eight in range(SLOTS // 8):
                    for tile in range(STEP // LANES):
                        line = index * (STEP // LANES * LOCAL) + line_of(row, tile)
                        lines[eight, pl.ds(line, 8, stride=PITCH), :] = value[
                            row * SLOTS + eight * 8 : row * SLOTS + eight * 8 + 8, tile * LANES : (tile + 1) * LANES
                        ]
            return inner

        lax.fori_loop(0, WIDTH // STEP, columns_step, 0)

        def pack(eight, inner):
            pack_eight(lines.at[eight], sent, half * SLOTS + eight * 8)
            return inner

        lax.fori_loop(0, SLOTS // 8, pack, 0)
        return carry

    def give_back(index, carry):
        target = moved(index, -1)
        pltpu.make_async_remote_copy(
            src_ref=sent.at[index], dst_ref=returned.at[place], send_sem=back_out_sem,
            recv_sem=back_sems.at[place // GROUP], device_id=(target, core), device_id_type=MESH,
        ).start()
        return carry

    gone = sent.at[pl.ds(1, CHIPS - 1)]
    pltpu.make_async_copy(gone, gone, out_sem).wait()
    finish(0, 0)
    pltpu.make_async_copy(sent.at[0], returned.at[place], back_sems.at[place // GROUP]).start()
    lax.fori_loop(1, SLOTS, give_back, 0)
    finish(1, 0)
    lax.fori_loop(SLOTS, CHIPS, give_back, 0)

    def collect(group, carry):
        span = returned.at[pl.ds(group * GROUP, GROUP)]
        pltpu.make_async_copy(span, span, back_sems.at[group]).wait()
        for eight in range(2):
            unpack_eight(lines.at[eight], returned, group * GROUP + eight * 8)
        rows = pl.ds(pl.multiple_of(group * GROUP, GROUP), GROUP)
        for row in range(LOCAL):
            for tile in range(TILES):
                values = [read_lines(lines.at[eight], row, tile) for eight in range(2)]
                update[row, rows, tile * LANES : (tile + 1) * LANES] = jnp.concatenate(values, axis=0).astype(
                    jnp.bfloat16
                )
        return carry

    lax.fori_loop(0, GROUPS, collect, 0)
    pltpu.make_async_copy(gone, gone, back_out_sem).wait()


def on_device(momentum, gradient, assignment):
    shape = (LOCAL, CHIPS, WIDTH)
    blocks = pltpu.VMEM((CHIPS, *BLOCK), jnp.bfloat16)
    momentum_new, update = pl.pallas_call(
        kernel,
        out_shape=(
            jax.ShapeDtypeStruct(shape, jnp.float32),
            jax.ShapeDtypeStruct(shape, jnp.bfloat16),
        ),
        in_specs=[
            pl.BlockSpec(memory_space=pl.ANY),
            pl.BlockSpec(memory_space=pl.ANY),
            pl.BlockSpec(memory_space=pltpu.SMEM),
        ],
        out_specs=[pl.BlockSpec(memory_space=pltpu.VMEM)] * 2,
        scratch_shapes=[
            pltpu.VMEM((GROUPS, LOCAL, GROUP, WIDTH), jnp.float32),
            pltpu.VMEM((GROUPS, LOCAL, GROUP, WIDTH), jnp.bfloat16),
            blocks,
            blocks,
            blocks,
            pltpu.VMEM((ROWS, WIDTH), jnp.bfloat16),
            pltpu.VMEM((ROWS, WIDTH), jnp.bfloat16),
            pltpu.VMEM((ROWS, ROWS), jnp.float32),
            pltpu.VMEM((ROWS, ROWS), jnp.bfloat16),
            pltpu.VMEM((ROWS, ROWS), jnp.bfloat16),
            pltpu.VMEM((SLOTS // 8, 8 * PITCH, LANES), jnp.float32),
            pltpu.VMEM((8, LANES), jnp.float32),
            pltpu.VMEM((8, LANES), jnp.float32),
            pltpu.SemaphoreType.DMA((2, GROUPS)),
            pltpu.SemaphoreType.DMA,
            pltpu.SemaphoreType.DMA((GROUPS,)),
            pltpu.SemaphoreType.DMA,
            pltpu.SemaphoreType.DMA((GROUPS,)),
            pltpu.SemaphoreType.DMA,
            pltpu.SemaphoreType.DMA((1,)),
            pltpu.SemaphoreType.DMA((2,)),
        ],
        compiler_params=pltpu.CompilerParams(
            collective_id=0, has_side_effects=True, vmem_limit_bytes=56 * 2**20
        ),
        name="muon",
    )(jnp.transpose(momentum, (1, 0, 2)), jnp.transpose(gradient, (1, 0, 2)), assignment)
    return jnp.transpose(momentum_new, (1, 0, 2)), jnp.transpose(update, (1, 0, 2))


def solution(mesh):
    placed = P(None, ("dp", "tensor"), None)
    return jax.shard_map(
        on_device,
        mesh=mesh,
        in_specs=(placed, placed, P()),
        out_specs=(placed, placed),
        check_vma=False,
    )
```

time: 213 us -> 88 us (0.41)
  Pallas kernels: 0 us -> 81.4 us
  waiting for transfers between devices: 81.3 us -> 0 us
  blocking collectives: 51 us -> 0 us
  matrix products: 22.8 us -> 0 us
  between operations: 14.5 us -> 0.65 us
  other arithmetic: 13.7 us -> 0 us
  local copies, waits for them, and re-layouts: 18.3 us -> 5.87 us
  starting transfers between devices: 10.5 us -> 0 us
    pallas_call x0 -> x1, Pallas kernels: none -> 81.4 us  [on_device(): pl.pallas_call(kernel, out_shape=(jax.ShapeDtypeStruct(shape, jnp.float32...]
    all_gather x4 -> x0, waiting for transfers between devices: 54 us -> none  [the longest x2 27.2 us: newton_schulz(): whole_rows = lax.all_gather(matrix_part, 'tensor', axis=1, tiled=True)]
    all_to_all x1 -> x0, blocking collectives: 45.7 us -> none  [on_device(): lax.all_to_all(direction, 'dp', split_axis=0, concat_axis=0, tiled=True)]
    all_to_all x1 -> x0, waiting for transfers between devices: 27.2 us -> none  [orthogonalize(): lax.all_to_all(result.reshape(item_count, source_count, row_count, col_co...]
    dot_general x4 -> x0, matrix products: 22.8 us -> none  [the longest x2 12.3 us: newton_schulz(): jnp.einsum('kij,kjd->kid', mixer_rows, whole_rows, preferred_element_type...]
    convert_element_type x3 -> x0, other arithmetic: 11.7 us -> none  [the longest x1 8.88 us: on_device(): direction = (wide + momentum_rate * momentum_new).astype(jnp.bfloat16)]
    all_to_all x1 -> x0, starting transfers between devices: 10.1 us -> none  [orthogonalize(): lax.all_to_all(result.reshape(item_count, source_count, row_count, col_co...]
    psum x1 -> x0, blocking collectives: 5.29 us -> none  [orthogonalize(): totals = lax.psum(squares, 'tensor')]
  transfers between devices with their start and end apart: 5 -> 0, of which waited for: 5 -> 0; matrix products, arithmetic and copies ran while one was open for 4% -> 0% of each run, Pallas kernels for 0% -> 0%
where the time goes in v2:
time: 88 us; the launch traced here: 87.9 us
  Pallas kernels  81.4 us (93%)
  local copies, waits for them, and re-layouts  5.87 us (7%)
    pallas_call x1, Pallas kernels, on_device(): pl.pallas_call(kernel, out_shape=(jax.ShapeDtypeStruct(shape, jnp.float32...  81.4 us
    unnamed x4, local copies, waits for them, and re-layouts  5.87 us

profile of v2, /device:TPU:1, one launch (start us, length us, event | category | flops | bytes accessed | tf_op | source)
XLA Modules:
  0.0 87.9 jit_solution(8156878995649536631)
XLA Ops:
  0.6 81.4 %muon.1 = (f32[6,64,2560]{2,1,0:T(8,128)}, bf16[6,64,2560]{2,1,0:T(8,128)(2,1)}) custom-call(f32[6,64,2560]{2,1,0:T(8,128)} %bitcast.4, bf16[6,64,2560]{2,1,0:T(8,128)(2,1)} %bitcast.6, s32[64]{0:T(128)} %assignment.1), custom_call_target="tpu_custom_call" | custom-call | tf_op jit(solution)/shard_map/muon/pallas_call | solution.py:310
  82.0 0.0 copy-start
  82.0 4.6 %copy.7 = f32[64,6,2560]{2,0,1:T(8,128)} copy(f32[64,6,2560]{2,0,1:T(8,128)} %bitcast.5) | data formatting | bytes 7864320
  86.6 0.0 copy-done
  86.6 1.3 %copy.8 = bf16[64,6,2560]{2,0,1:T(8,128)(2,1)} copy(bf16[64,6,2560]{2,0,1:T(8,128)(2,1)S(1)} %bitcast.7) | data formatting | bytes 3932160
Async XLA Ops:
  82.0 4.6 %copy-start = (bf16[6,64,2560]{2,1,0:T(8,128)(2,1)S(1)}, bf16[6,64,2560]{2,1,0:T(8,128)(2,1)}, u32[]{:S(2)}) copy-start(bf16[6,64,2560]{2,1,0:T(8,128)(2,1)} %get-tuple-element.5) | copy-start | bytes 5898244

commit v3 on v2

--- a/solution.py
+++ b/solution.py
@@ -30,27 +30,39 @@
 PITCH = LINES + 1
 GROUP = 16
 GROUPS = CHIPS // GROUP
-HALVES = 2
-SLOTS = CHIPS // HALVES
+SHARES = 4
+SLOTS = CHIPS // SHARES
 STEP = 512
 TILE = 256
 STRIPS = ROWS // TILE
-STRIDE = 27
 
 
 def position():
     return lax.axis_index("dp"), lax.axis_index("tensor")
 
 
-def moved(index, sign):
+def spread_offsets():
+    sets = []
+    for offset in ((x, y, z) for x in range(SIDE) for y in range(SIDE) for z in range(SIDE)):
+        turns = [offset[turn:] + offset[:turn] for turn in range(3)]
+        alike = dict.fromkeys(tuple(sign * step % SIDE for step in turn) for sign in (1, -1) for turn in turns)
+        if offset == min(alike):
+            sets.append(list(alike))
+    hops = [sum(min(step, SIDE - step) for step in alike[0]) for alike in sets]
+    ranked = sorted(range(1, len(sets)), key=lambda index: -hops[index])
+    return [offset for index in [0, *ranked] for offset in sets[index]]
+
+
+OFFSETS = spread_offsets()
+
+
+def targets(sign):
     place, _ = position()
-    offset = index * STRIDE % CHIPS
-    spot = 0
+    steps = []
     for scale in (SIDE * SIDE, SIDE, 1):
         here = place // scale % SIDE
-        away = offset // scale % SIDE
-        spot = spot + (here + sign * away + SIDE) % SIDE * scale
-    return spot
+        steps.append([(here + sign * away + SIDE) % SIDE * scale for away in range(SIDE)])
+    return [steps[0][x] + steps[1][y] + steps[2][z] for x, y, z in OFFSETS]
 
 
 def line_of(row, tile):
@@ -98,14 +110,13 @@
                 low[strip(j), strip(i)] = value.T.astype(jnp.bfloat16)
 
 
-def mixer_of(gram, low, mixer):
-    for j in range(STRIPS):
-        for i in range(j, STRIPS):
-            square = product(low[strip(i), :], low[:, strip(j)], ((1,), (0,)))
-            value = cubic_term * gram[strip(i), strip(j)] + quintic_term * square
-            mixer[strip(i), strip(j)] = value.astype(jnp.bfloat16)
-            if i != j:
-                mixer[strip(j), strip(i)] = value.T.astype(jnp.bfloat16)
+def mixer_of(gram, low, mixer, j):
+    for i in range(j, STRIPS):
+        square = product(low[strip(i), :], low[:, strip(j)], ((1,), (0,)))
+        value = cubic_term * gram[strip(i), strip(j)] + quintic_term * square
+        mixer[strip(i), strip(j)] = value.astype(jnp.bfloat16)
+        if i != j:
+            mixer[strip(j), strip(i)] = value.T.astype(jnp.bfloat16)
 
 
 def kernel(
@@ -130,11 +141,9 @@
     barrier = pltpu.get_barrier_semaphore()
     pl.semaphore_signal(barrier, inc=1, device_id=pair, device_id_type=MESH)
 
-    def greet(index, carry):
-        pl.semaphore_signal(barrier, inc=1, device_id=(moved(index, 1), core), device_id_type=MESH)
-        return carry
-
-    lax.fori_loop(1, CHIPS, greet, 0)
+    ahead = targets(1)
+    for target in ahead[1:]:
+        pl.semaphore_signal(barrier, inc=1, device_id=(target, core), device_id_type=MESH)
 
     def prepare(group, carry):
         for copy in load(group):
@@ -159,19 +168,15 @@
 
     pltpu.make_async_copy(sent.at[place], arrived.at[0], in_sems.at[0]).start()
 
-    def send(index, carry):
-        target = moved(index, 1)
-        pltpu.make_async_remote_copy(
-            src_ref=sent.at[target], dst_ref=arrived.at[index], send_sem=out_sem, recv_sem=in_sems.at[index // GROUP],
-            device_id=(target, core), device_id_type=MESH,
-        ).start()
-        return carry
-
-    lax.fori_loop(1, CHIPS, send, 0)
+    for slot, target in enumerate(ahead):
+        if slot:
+            pltpu.make_async_remote_copy(
+                src_ref=sent.at[target], dst_ref=arrived.at[slot], send_sem=out_sem, recv_sem=in_sems.at[slot // GROUP],
+                device_id=(target, core), device_id_type=MESH,
+            ).start()
 
     def rows_of(group, row):
-        start = group // (GROUPS // HALVES) * (LOCAL * SLOTS) + row * SLOTS + group % (GROUPS // HALVES) * GROUP
-        return pl.multiple_of(start, GROUP)
+        return pl.multiple_of(group * (LOCAL * GROUP) + row * GROUP, GROUP)
 
     def relay(group, row):
         start = rows_of(group, row)
@@ -223,7 +228,8 @@
     lax.fori_loop(0, ROWS // 32, normalize, 0)
 
     gram_of(x_now, gram, low)
-    mixer_of(gram, low, mixer)
+    for j in range(STRIPS):
+        mixer_of(gram, low, mixer, j)
 
     def mix(index, carry):
         columns = pl.ds(pl.multiple_of(index * STEP, STEP), STEP)
@@ -237,15 +243,14 @@
     lax.fori_loop(0, WIDTH // STEP, mix, 0)
 
     gram_of(x_next, gram, low)
-    mixer_of(gram, low, mixer)
 
     active = assignment[place] >= 0
     part = LOCAL * SLOTS
 
-    def finish(half, carry):
-        rows = pl.ds(pl.multiple_of(half * part, part), part)
-
-        def columns_step(index, inner):
+    def finish(share):
+        rows = slice(share * part, (share + 1) * part)
+
+        def columns_step(index, carry):
             columns = pl.ds(pl.multiple_of(index * STEP, STEP), STEP)
             value = linear_term * x_next[rows, columns].astype(jnp.float32) + product(
                 mixer[rows, :], x_next[:, columns], ((1,), (0,))
@@ -254,37 +259,34 @@
             value = jnp.where(active, value, 0.0)
             for row in range(LOCAL):
                 for eight in range(SLOTS // 8):
+                    start = row * SLOTS + eight * 8
                     for tile in range(STEP // LANES):
                         line = index * (STEP // LANES * LOCAL) + line_of(row, tile)
                         lines[eight, pl.ds(line, 8, stride=PITCH), :] = value[
-                            row * SLOTS + eight * 8 : row * SLOTS + eight * 8 + 8, tile * LANES : (tile + 1) * LANES
+                            start : start + 8, tile * LANES : (tile + 1) * LANES
                         ]
-            return inner
+            return carry
 
         lax.fori_loop(0, WIDTH // STEP, columns_step, 0)
-
-        def pack(eight, inner):
-            pack_eight(lines.at[eight], sent, half * SLOTS + eight * 8)
-            return inner
-
-        lax.fori_loop(0, SLOTS // 8, pack, 0)
-        return carry
-
-    def give_back(index, carry):
-        target = moved(index, -1)
-        pltpu.make_async_remote_copy(
-            src_ref=sent.at[index], dst_ref=returned.at[place], send_sem=back_out_sem,
-            recv_sem=back_sems.at[place // GROUP], device_id=(target, core), device_id_type=MESH,
-        ).start()
-        return carry
+        for eight in range(SLOTS // 8):
+            pack_eight(lines.at[eight], sent, share * SLOTS + eight * 8)
 
     gone = sent.at[pl.ds(1, CHIPS - 1)]
     pltpu.make_async_copy(gone, gone, out_sem).wait()
-    finish(0, 0)
-    pltpu.make_async_copy(sent.at[0], returned.at[place], back_sems.at[place // GROUP]).start()
-    lax.fori_loop(1, SLOTS, give_back, 0)
-    finish(1, 0)
-    lax.fori_loop(SLOTS, CHIPS, give_back, 0)
+    behind = targets(-1)
+    for share in range(SHARES):
+        for j in range(STRIPS):
+            if share * part <= j * TILE < (share + 1) * part:
+                mixer_of(gram, low, mixer, j)
+        finish(share)
+        for slot in range(share * SLOTS, (share + 1) * SLOTS):
+            if slot == 0:
+                pltpu.make_async_copy(sent.at[0], returned.at[place], back_sems.at[place // GROUP]).start()
+            else:
+                pltpu.make_async_remote_copy(
+                    src_ref=sent.at[slot], dst_ref=returned.at[place], send_sem=back_out_sem,
+                    recv_sem=back_sems.at[place // GROUP], device_id=(behind[slot], core), device_id_type=MESH,
+                ).start()
 
     def collect(group, carry):
         span = returned.at[pl.ds(group * GROUP, GROUP)]
@@ -310,8 +312,8 @@
     momentum_new, update = pl.pallas_call(
         kernel,
         out_shape=(
-            jax.ShapeDtypeStruct(shape, jnp.float32),
-            jax.ShapeDtypeStruct(shape, jnp.bfloat16),
+            pltpu.VMEM(shape, jnp.float32),
+            pltpu.VMEM(shape, jnp.bfloat16),
         ),
         in_specs=[
             pl.BlockSpec(memory_space=pl.ANY),

time: 88 us -> 78.5 us (0.89)
  Pallas kernels: 81.4 us -> 74.5 us
  local copies, waits for them, and re-layouts: 5.87 us -> 3.2 us
    pallas_call x1, Pallas kernels: 81.4 us -> 74.5 us  [on_device(): pl.pallas_call(kernel, out_shape=(pltpu.VMEM(shape, jnp.float32), pltpu.V...]
    unnamed x4 -> x2, local copies, waits for them, and re-layouts: 5.87 us -> 3.2 us
where the time goes in v3:
time: 78.5 us; the launch traced here: 78.4 us
  Pallas kernels  74.5 us (95%)
  local copies, waits for them, and re-layouts  3.2 us (4%)
    pallas_call x1, Pallas kernels, on_device(): pl.pallas_call(kernel, out_shape=(pltpu.VMEM(shape, jnp.float32), pltpu.V...  74.5 us
    unnamed x2, local copies, waits for them, and re-layouts  3.2 us

profile of v3, /device:TPU:1, one launch (start us, length us, event | category | flops | bytes accessed | tf_op | source)
XLA Modules:
  0.0 78.4 jit_solution(3763682218336492677)
XLA Ops:
  0.6 74.5 %muon.1 = (f32[6,64,2560]{2,1,0:T(8,128)S(1)}, bf16[6,64,2560]{2,1,0:T(8,128)(2,1)S(1)}) custom-call(f32[6,64,2560]{2,1,0:T(8,128)} %bitcast.6, bf16[6,64,2560]{2,1,0:T(8,128)(2,1)} %bitcast.7, s32[64]{0:T(128)} %assignment.1), custom_call_target="tpu_custom_call" | custom-call | tf_op jit(solution)/shard_map/muon/pallas_call | solution.py:312
  75.2 1.9 %copy.7 = f32[64,6,2560]{2,0,1:T(8,128)} copy(f32[64,6,2560]{2,0,1:T(8,128)S(1)} %bitcast.4) | data formatting | bytes 7864320
  77.1 1.3 %copy.8 = bf16[64,6,2560]{2,0,1:T(8,128)(2,1)} copy(bf16[64,6,2560]{2,0,1:T(8,128)(2,1)S(1)} %bitcast.5) | data formatting | bytes 3932160

commit v4 on v3

v4 whole, which is shorter than its diff:
```python
import math

import jax
import jax.numpy as jnp
from jax import lax
from jax.experimental import pallas as pl
from jax.experimental.pallas import tpu as pltpu
from jax.sharding import PartitionSpec as P

ITERS = 2
MESH = pl.DeviceIdType.MESH

momentum_rate = 0.95
epsilon_norm = 1e-07
linear_term = 3.4445
cubic_term = -4.775
quintic_term = 2.0315

SIDE = 4
CHIPS = SIDE**3
LOCAL = 6
WIDTH = 2560
LANES = 128
TILES = WIDTH // LANES
ROWS = LOCAL * CHIPS * 2
HALF = LOCAL * CHIPS
LINES = LOCAL * TILES
BLOCK = (8, LINES // 8 * LANES)
PITCH = LINES + 1
GROUP = 16
GROUPS = CHIPS // GROUP
PIECE = 4
PIECES = CHIPS // PIECE
SHARES = ((0, 1), (1, GROUPS))
TILE = 256
STRIPS = ROWS // TILE


def position():
    return lax.axis_index("dp"), lax.axis_index("tensor")


def spread_offsets():
    sets = []
    for offset in ((x, y, z) for x in range(SIDE) for y in range(SIDE) for z in range(SIDE)):
        turns = [offset[turn:] + offset[:turn] for turn in range(3)]
        alike = dict.fromkeys(tuple(sign * step % SIDE for step in turn) for sign in (1, -1) for turn in turns)
        if offset == min(alike):
            sets.append(list(alike))
    hops = [sum(min(step, SIDE - step) for step in alike[0]) for alike in sets]
    ranked = sorted(range(1, len(sets)), key=lambda index: -hops[index])
    return [offset for index in [0, *ranked] for offset in sets[index]]


OFFSETS = spread_offsets()


def targets(sign):
    place, _ = position()
    steps = []
    for scale in (SIDE * SIDE, SIDE, 1):
        here = place // scale % SIDE
        steps.append([(here + sign * away + SIDE) % SIDE * scale for away in range(SIDE)])
    return [steps[0][x] + steps[1][y] + steps[2][z] for x, y, z in OFFSETS]


def line_of(row, tile):
    return tile * LOCAL + row


def write_lines(scratch, row, tile, values):
    scratch[pl.ds(line_of(row, tile), 8, stride=PITCH), :] = values


def read_lines(scratch, row, tile):
    return scratch[pl.ds(line_of(row, tile), 8, stride=PITCH), :]


def pack_eight(scratch, blocks, first):
    for item in range(8):
        for part in range(LINES // 8):
            values = scratch[pl.ds(item * PITCH + 8 * part, 8), :]
            blocks[first + item, :, part * LANES : (part + 1) * LANES] = values.astype(jnp.bfloat16)


def unpack_eight(scratch, blocks, first):
    for item in range(8):
        values = blocks[first + item].astype(jnp.float32)
        for part in range(LINES // 8):
            scratch[pl.ds(item * PITCH + 8 * part, 8), :] = values[:, part * LANES : (part + 1) * LANES]


def product(a, b, dims):
    return lax.dot_general(a, b, (dims, ((), ())), preferred_element_type=jnp.float32)


def strip(index):
    return slice(index * TILE, (index + 1) * TILE)


def gram_block(x_ref, i, j):
    return product(x_ref[strip(i), :], x_ref[strip(j), :], ((1,), (1,)))


def keep_block(gram, low, i, j, value):
    gram[strip(i), strip(j)] = value
    low[strip(i), strip(j)] = value.astype(jnp.bfloat16)
    if i != j:
        low[strip(j), strip(i)] = value.T.astype(jnp.bfloat16)


def lay_out(lines, blocks, group, write):
    for eight in range(2):
        unpack_eight(lines.at[eight], blocks, group * GROUP + eight * 8)
    for row in range(LOCAL):
        for tile in range(TILES):
            values = [read_lines(lines.at[eight], row, tile) for eight in range(2)]
            write(row, tile, jnp.concatenate(values, axis=0).astype(jnp.bfloat16))


def share_rows(group, core=0):
    return (2 * group + core) * LOCAL * GROUP


def mixer_of(gram, low, mixer, j):
    for i in range(j, STRIPS):
        square = product(low[strip(i), :], low[:, strip(j)], ((1,), (0,)))
        value = cubic_term * gram[strip(i), strip(j)] + quintic_term * square
        mixer[strip(i), strip(j)] = value.astype(jnp.bfloat16)
        if i != j:
            mixer[strip(j), strip(i)] = value.T.astype(jnp.bfloat16)


def kernel(
    momentum, gradient, assignment, momentum_new, returned,
    mom_in, grad_in, sent, arrived, relayed, x_now, x_next, gram, low, mixer, lines,
    load_sems, out_sem, in_sems, back_out_sem, back_sem, pair_out_sem, pair_sems,
):
    place, core = position()
    pair = (place, 1 - core)

    def load(group):
        rows = pl.ds(pl.multiple_of(group * GROUP, GROUP), GROUP)
        return (
            pltpu.make_async_copy(momentum.at[:, rows, :], mom_in.at[group], load_sems.at[0, group]),
            pltpu.make_async_copy(gradient.at[:, rows, :], grad_in.at[group], load_sems.at[1, group]),
        )

    for group in range(GROUPS):
        for copy in load(group):
            copy.start()

    barrier = pltpu.get_barrier_semaphore()
    pl.semaphore_signal(barrier, inc=1, device_id=pair, device_id_type=MESH)

    ahead = targets(1)
    for target in ahead[1:]:
        pl.semaphore_signal(barrier, inc=1, device_id=(target, core), device_id_type=MESH)

    def prepare(group, carry):
        for copy in load(group):
            copy.wait()
        rows = pl.ds(pl.multiple_of(group * GROUP, GROUP), GROUP)
        for row in range(LOCAL):
            for tile in range(TILES):
                columns = slice(tile * LANES, (tile + 1) * LANES)
                wide = grad_in[group, row, :, columns].astype(jnp.float32)
                fresh = momentum_rate * mom_in[group, row, :, columns] + wide
                momentum_new[row, rows, columns] = fresh
                direction = wide + momentum_rate * fresh
                for eight in range(2):
                    write_lines(lines.at[eight], row, tile, direction[eight * 8 : eight * 8 + 8])
        for eight in range(2):
            pack_eight(lines.at[eight], sent, group * GROUP + eight * 8)
        return carry

    lax.fori_loop(0, GROUPS, prepare, 0)

    pl.semaphore_wait(barrier, CHIPS)

    pltpu.make_async_copy(sent.at[place], arrived.at[0], in_sems.at[0]).start()

    for slot, target in enumerate(ahead):
        if slot:
            pltpu.make_async_remote_copy(
                src_ref=sent.at[target], dst_ref=arrived.at[slot], send_sem=out_sem, recv_sem=in_sems.at[slot // PIECE],
                device_id=(target, core), device_id_type=MESH,
            ).start()

    def accept(blocks, group, which):
        def write(row, tile, values):
            start = share_rows(group, which) + row * GROUP
            x_now[start : start + GROUP, tile * LANES : (tile + 1) * LANES] = values

        lay_out(lines, blocks, group, write)

    def accept_pair(group):
        span = relayed.at[pl.ds(group * GROUP, GROUP)]
        pltpu.make_async_copy(span, span, pair_sems.at[group]).wait()
        accept(relayed, group, 1)
        for i in range(STRIPS):
            if share_rows(group) < (i + 1) * TILE <= share_rows(group + 1):
                for j in range(i + 1):
                    gram[strip(i), strip(j)] = gram_block(x_now, i, j)

    for group in range(GROUPS):
        if group:
            accept_pair(group - 1)
        for piece in range(group * GROUP // PIECE, (group + 1) * GROUP // PIECE):
            span = pl.ds(piece * PIECE, PIECE)
            pltpu.make_async_copy(arrived.at[span], arrived.at[span], in_sems.at[piece]).wait()
            pltpu.make_async_remote_copy(
                src_ref=arrived.at[span], dst_ref=relayed.at[span], send_sem=pair_out_sem, recv_sem=pair_sems.at[group],
                device_id=pair, device_id_type=MESH,
            ).start()
        accept(arrived, group, 0)
    accept_pair(GROUPS - 1)

    diagonal = lax.broadcasted_iota(jnp.int32, (TILE, TILE), 0) == lax.broadcasted_iota(jnp.int32, (TILE, TILE), 1)
    total = jnp.zeros((TILE, TILE), jnp.float32)
    for i in range(STRIPS):
        total += jnp.where(diagonal, gram[strip(i), strip(i)], 0.0)
    total = jnp.sum(total)
    scale = 1.0 / (jnp.sqrt(total) + epsilon_norm)
    for i in range(STRIPS):
        for j in range(i + 1):
            value = jnp.where(scale > 0.0, gram[strip(i), strip(j)] * scale * scale, 0.0)
            keep_block(gram, low, i, j, value)

    def normalize(part):
        rows = slice(part * LANES, (part + 1) * LANES)
        x_now[rows, :] = (x_now[rows, :].astype(jnp.float32) * scale).astype(jnp.bfloat16)

    for j in range(STRIPS):
        mixer_of(gram, low, mixer, j)
        normalize(2 * j)
        normalize(2 * j + 1)

    for i in range(STRIPS):
        value = product(mixer[strip(i), :], x_now[...], ((1,), (0,)))
        x_next[strip(i), :] = (linear_term * x_now[strip(i), :].astype(jnp.float32) + value).astype(jnp.bfloat16)

    for i in range(STRIPS):
        for j in range(i + 1):
            keep_block(gram, low, i, j, gram_block(x_next, i, j))

    active = assignment[place] >= 0
    made = set()

    def finish(first, last):
        for group in range(first, last):
            for j in range(STRIPS):
                if j not in made and share_rows(group) < (j + 1) * TILE and j * TILE < share_rows(group, 1):
                    made.add(j)
                    mixer_of(gram, low, mixer, j)
        rows = [slice(share_rows(group), share_rows(group, 1)) for group in range(first, last)]

        def gathered(ref):
            parts = [ref[row, :] for row in rows]
            return parts[0] if len(parts) == 1 else jnp.concatenate(parts, axis=0)

        value = linear_term * gathered(x_next).astype(jnp.float32) + product(
            gathered(mixer), x_next[...], ((1,), (0,))
        )
        value = math.sqrt(WIDTH) * value.astype(jnp.bfloat16).astype(jnp.float32)
        value = jnp.where(active, value, 0.0)
        for group in range(first, last):
            for eight in range(2):
                place_lines = lines.at[2 * (group - first) + eight]
                for row in range(LOCAL):
                    start = (group - first) * LOCAL * GROUP + row * GROUP + eight * 8
                    for tile in range(TILES):
                        write_lines(
                            place_lines, row, tile, value[start : start + 8, tile * LANES : (tile + 1) * LANES]
                        )
                pack_eight(place_lines, sent, group * GROUP + eight * 8)

    gone = sent.at[pl.ds(1, CHIPS - 1)]
    pltpu.make_async_copy(gone, gone, out_sem).wait()
    behind = targets(-1)
    for first, last in SHARES:
        finish(first, last)
        for slot in range(first * GROUP, last * GROUP):
            if slot == 0:
                pltpu.make_async_copy(sent.at[0], returned.at[place], back_sem).start()
            else:
                pltpu.make_async_remote_copy(
                    src_ref=sent.at[slot], dst_ref=returned.at[place], send_sem=back_out_sem, recv_sem=back_sem,
                    device_id=(behind[slot], core), device_id_type=MESH,
                ).start()

    pltpu.make_async_copy(arrived, arrived, pair_out_sem).wait()
    pltpu.make_async_copy(returned, returned, back_sem).wait()
    pltpu.make_async_copy(gone, gone, back_out_sem).wait()


def place_results(fresh, returned, momentum_new, update, rows_out, lines, fresh_sem, group_sems):
    whole = pltpu.make_async_copy(fresh, momentum_new, fresh_sem)
    whole.start()
    copies = []
    for group in range(GROUPS):
        rows = pl.ds(group * GROUP, GROUP)

        def write(row, tile, values):
            rows_out[row, group * GROUP : (group + 1) * GROUP, tile * LANES : (tile + 1) * LANES] = values

        lay_out(lines, returned, group, write)
        copies.append(
            pltpu.make_async_copy(rows_out.at[:, rows, :], update.at[:, rows, :], group_sems.at[group])
        )
        copies[-1].start()
    for copy in copies:
        copy.wait()
    whole.wait()


def on_device(momentum, gradient, assignment):
    shape = (LOCAL, CHIPS, WIDTH)
    blocks = pltpu.VMEM((CHIPS, *BLOCK), jnp.bfloat16)
    line_space = pltpu.VMEM((2 * GROUPS, 8 * PITCH, LANES), jnp.float32)
    fresh, returned = pl.pallas_call(
        kernel,
        out_shape=(pltpu.VMEM(shape, jnp.float32), blocks),
        in_specs=[
            pl.BlockSpec(memory_space=pl.ANY),
            pl.BlockSpec(memory_space=pl.ANY),
            pl.BlockSpec(memory_space=pltpu.SMEM),
        ],
        out_specs=[pl.BlockSpec(memory_space=pltpu.VMEM)] * 2,
        scratch_shapes=[
            pltpu.VMEM((GROUPS, LOCAL, GROUP, WIDTH), jnp.float32),
            pltpu.VMEM((GROUPS, LOCAL, GROUP, WIDTH), jnp.bfloat16),
            blocks,
            blocks,
            blocks,
            pltpu.VMEM((ROWS, WIDTH), jnp.bfloat16),
            pltpu.VMEM((ROWS, WIDTH), jnp.bfloat16),
            pltpu.VMEM((ROWS, ROWS), jnp.float32),
            pltpu.VMEM((ROWS, ROWS), jnp.bfloat16),
            pltpu.VMEM((ROWS, ROWS), jnp.bfloat16),
            line_space,
            pltpu.SemaphoreType.DMA((2, GROUPS)),
            pltpu.SemaphoreType.DMA,
            pltpu.SemaphoreType.DMA((PIECES,)),
            pltpu.SemaphoreType.DMA,
            pltpu.SemaphoreType.DMA,
            pltpu.SemaphoreType.DMA,
            pltpu.SemaphoreType.DMA((GROUPS,)),
        ],
        compiler_params=pltpu.CompilerParams(
            collective_id=0, has_side_effects=True, vmem_limit_bytes=50 * 2**20
        ),
        name="muon",
    )(jnp.transpose(momentum, (1, 0, 2)), jnp.transpose(gradient, (1, 0, 2)), assignment)
    momentum_new, update = pl.pallas_call(
        place_results,
        out_shape=(jax.ShapeDtypeStruct(shape, jnp.float32), jax.ShapeDtypeStruct(shape, jnp.bfloat16)),
        in_specs=[pl.BlockSpec(memory_space=pltpu.VMEM)] * 2,
        out_specs=[pl.BlockSpec(memory_space=pl.ANY)] * 2,
        scratch_shapes=[
            pltpu.VMEM(shape, jnp.bfloat16),
            line_space,
            pltpu.SemaphoreType.DMA,
            pltpu.SemaphoreType.DMA((GROUPS,)),
        ],
        compiler_params=pltpu.CompilerParams(vmem_limit_bytes=32 * 2**20),
        name="place_results",
    )(fresh, returned)
    return jnp.transpose(momentum_new, (1, 0, 2)), jnp.transpose(update, (1, 0, 2))


def solution(mesh):
    placed = P(None, ("dp", "tensor"), None)
    return jax.shard_map(
        on_device,
        mesh=mesh,
        in_specs=(placed, placed, P()),
        out_specs=(placed, placed),
        check_vma=False,
    )
```

time: 78.5 us -> 78.1 us (level)
  local copies, waits for them, and re-layouts: 3.2 us -> 0 us
  Pallas kernels: 74.5 us -> 77.2 us
    unnamed x2 -> x0, local copies, waits for them, and re-layouts: 3.2 us -> none
    pallas_call x1 -> x2, Pallas kernels: 74.5 us -> 77.2 us  [the longest x1 74.6 us: on_device(): pl.pallas_call(kernel, out_shape=(pltpu.VMEM(shape, jnp.float32), blocks)...]
where the time goes in v4:
time: 78.1 us; the launch traced here: 78 us
  Pallas kernels  77.2 us (99%)
  between operations  0.8 us (1%)
    pallas_call x1, Pallas kernels, on_device(): pl.pallas_call(kernel, out_shape=(pltpu.VMEM(shape, jnp.float32), blocks)...  74.6 us
    pallas_call x1, Pallas kernels, on_device(): pl.pallas_call(place_results, out_shape=(jax.ShapeDtypeStruct(shape, jnp....  2.58 us

profile of v4, /device:TPU:1, one launch (start us, length us, event | category | flops | bytes accessed | tf_op | source)
XLA Modules:
  0.0 78.0 jit_solution(9587622074362098640)
XLA Ops:
  0.6 74.6 %muon.1 = (f32[6,64,2560]{2,1,0:T(8,128)S(1)}, bf16[64,8,1920]{2,1,0:T(8,128)(2,1)S(1)}) custom-call(f32[6,64,2560]{2,1,0:T(8,128)} %bitcast.4, bf16[6,64,2560]{2,1,0:T(8,128)(2,1)} %bitcast.5, s32[64]{0:T(128)} %assignment.1), custom_call_target="tpu_custom_call" | custom-call | tf_op jit(solution)/shard_map/muon/pallas_call | solution.py:321
  75.3 2.6 %place_results.1 = (f32[6,64,2560]{2,1,0:T(8,128)}, bf16[6,64,2560]{2,1,0:T(8,128)(2,1)}) custom-call(f32[6,64,2560]{2,1,0:T(8,128)S(1)} %get-tuple-element.6.fresh, bf16[64,8,1920]{2,1,0:T(8,128)(2,1)S(1)} %get-tuple-element.7.returned), custom_call_target="tpu_custom_call" | custom-call | tf_op jit(solution)/shard_map/place_results/pallas_call | solution.py:355

commit v5 on v4

--- a/solution.py
+++ b/solution.py
@@ -48,7 +48,13 @@
         if offset == min(alike):
             sets.append(list(alike))
     hops = [sum(min(step, SIDE - step) for step in alike[0]) for alike in sets]
-    ranked = sorted(range(1, len(sets)), key=lambda index: -hops[index])
+    ranked, rest = [], {}
+    for index in range(1, len(sets)):
+        rest.setdefault(hops[index], []).append(index)
+    while any(rest.values()):
+        for some in rest.values():
+            if some:
+                ranked.append(some.pop())
     return [offset for index in [0, *ranked] for offset in sets[index]]
 
 
@@ -109,13 +115,15 @@
         low[strip(j), strip(i)] = value.T.astype(jnp.bfloat16)
 
 
-def lay_out(lines, blocks, group, write):
+def lay_out(lines, blocks, group, write, sums=None):
     for eight in range(2):
         unpack_eight(lines.at[eight], blocks, group * GROUP + eight * 8)
     for row in range(LOCAL):
         for tile in range(TILES):
             values = [read_lines(lines.at[eight], row, tile) for eight in range(2)]
             write(row, tile, jnp.concatenate(values, axis=0).astype(jnp.bfloat16))
+            for index, value in enumerate(values if sums else ()):
+                sums[2 * (tile % 2) + index] += value * value
 
 
 def share_rows(group, core=0):
@@ -133,7 +141,7 @@
 
 def kernel(
     momentum, gradient, assignment, momentum_new, returned,
-    mom_in, grad_in, sent, arrived, relayed, x_now, x_next, gram, low, mixer, lines,
+    mom_in, grad_in, sent, arrived, relayed, x_now, x_next, gram, low, mixer, lines, squares,
     load_sems, out_sem, in_sems, back_out_sem, back_sem, pair_out_sem, pair_sems,
 ):
     place, core = position()
@@ -192,17 +200,20 @@
             start = share_rows(group, which) + row * GROUP
             x_now[start : start + GROUP, tile * LANES : (tile + 1) * LANES] = values
 
-        lay_out(lines, blocks, group, write)
+        sums = [jnp.zeros((8, LANES), jnp.float32)] * 4
+        lay_out(lines, blocks, group, write, sums)
+        squares[...] += (sums[0] + sums[1]) + (sums[2] + sums[3])
 
     def accept_pair(group):
         span = relayed.at[pl.ds(group * GROUP, GROUP)]
         pltpu.make_async_copy(span, span, pair_sems.at[group]).wait()
         accept(relayed, group, 1)
-        for i in range(STRIPS):
+        for i in range(STRIPS - 1):
             if share_rows(group) < (i + 1) * TILE <= share_rows(group + 1):
                 for j in range(i + 1):
                     gram[strip(i), strip(j)] = gram_block(x_now, i, j)
 
+    squares[...] = jnp.zeros_like(squares)
     for group in range(GROUPS):
         if group:
             accept_pair(group - 1)
@@ -216,29 +227,24 @@
         accept(arrived, group, 0)
     accept_pair(GROUPS - 1)
 
-    diagonal = lax.broadcasted_iota(jnp.int32, (TILE, TILE), 0) == lax.broadcasted_iota(jnp.int32, (TILE, TILE), 1)
-    total = jnp.zeros((TILE, TILE), jnp.float32)
-    for i in range(STRIPS):
-        total += jnp.where(diagonal, gram[strip(i), strip(i)], 0.0)
-    total = jnp.sum(total)
-    scale = 1.0 / (jnp.sqrt(total) + epsilon_norm)
-    for i in range(STRIPS):
-        for j in range(i + 1):
-            value = jnp.where(scale > 0.0, gram[strip(i), strip(j)] * scale * scale, 0.0)
-            keep_block(gram, low, i, j, value)
-
-    def normalize(part):
-        rows = slice(part * LANES, (part + 1) * LANES)
-        x_now[rows, :] = (x_now[rows, :].astype(jnp.float32) * scale).astype(jnp.bfloat16)
+    scale = 1.0 / (jnp.sqrt(jnp.sum(squares[...])) + epsilon_norm)
+
+    def scaled(value):
+        return jnp.where(scale > 0.0, value * scale * scale, 0.0)
+
+    before = [(i, j) for i in range(STRIPS - 1) for j in range(i + 1)]
+    for j in range(STRIPS):
+        keep_block(gram, low, STRIPS - 1, j, scaled(gram_block(x_now, STRIPS - 1, j)))
+        for i, k in before[j::STRIPS]:
+            keep_block(gram, low, i, k, scaled(gram[strip(i), strip(k)]))
 
     for j in range(STRIPS):
         mixer_of(gram, low, mixer, j)
-        normalize(2 * j)
-        normalize(2 * j + 1)
-
-    for i in range(STRIPS):
-        value = product(mixer[strip(i), :], x_now[...], ((1,), (0,)))
-        x_next[strip(i), :] = (linear_term * x_now[strip(i), :].astype(jnp.float32) + value).astype(jnp.bfloat16)
+
+    for index in range(WIDTH // TILE):
+        start = (x_now[:, strip(index)].astype(jnp.float32) * scale).astype(jnp.bfloat16)
+        value = product(mixer[...], start, ((1,), (0,)))
+        x_next[:, strip(index)] = (linear_term * start.astype(jnp.float32) + value).astype(jnp.bfloat16)
 
     for i in range(STRIPS):
         for j in range(i + 1):
@@ -339,6 +345,7 @@
             pltpu.VMEM((ROWS, ROWS), jnp.bfloat16),
             pltpu.VMEM((ROWS, ROWS), jnp.bfloat16),
             line_space,
+            pltpu.VMEM((8, LANES), jnp.float32),
             pltpu.SemaphoreType.DMA((2, GROUPS)),
             pltpu.SemaphoreType.DMA,
             pltpu.SemaphoreType.DMA((PIECES,)),

time: 78.1 us -> 75.3 us (0.964)
  Pallas kernels: 77.2 us -> 74.3 us
    pallas_call x1, Pallas kernels: 74.6 us -> 71.8 us  [on_device(): pl.pallas_call(kernel, out_shape=(pltpu.VMEM(shape, jnp.float32), blocks)...]
where the time goes in v5:
time: 75.3 us; the launch traced here: 75.1 us
  Pallas kernels  74.3 us (99%)
  between operations  0.8 us (1%)
    pallas_call x1, Pallas kernels, on_device(): pl.pallas_call(kernel, out_shape=(pltpu.VMEM(shape, jnp.float32), blocks)...  71.8 us
    pallas_call x1, Pallas kernels, on_device(): pl.pallas_call(place_results, out_shape=(jax.ShapeDtypeStruct(shape, jnp....  2.58 us

profile of v5, /device:TPU:1, one launch (start us, length us, event | category | flops | bytes accessed | tf_op | source)
XLA Modules:
  0.0 75.1 jit_solution(16515752296799648328)
XLA Ops:
  0.6 71.8 %muon.1 = (f32[6,64,2560]{2,1,0:T(8,128)S(1)}, bf16[64,8,1920]{2,1,0:T(8,128)(2,1)S(1)}) custom-call(f32[6,64,2560]{2,1,0:T(8,128)} %bitcast.4, bf16[6,64,2560]{2,1,0:T(8,128)(2,1)} %bitcast.5, s32[64]{0:T(128)} %assignment.1), custom_call_target="tpu_custom_call" | custom-call | tf_op jit(solution)/shard_map/muon/pallas_call | solution.py:327
  72.4 2.6 %place_results.1 = (f32[6,64,2560]{2,1,0:T(8,128)}, bf16[6,64,2560]{2,1,0:T(8,128)(2,1)}) custom-call(f32[6,64,2560]{2,1,0:T(8,128)S(1)} %get-tuple-element.6.fresh, bf16[64,8,1920]{2,1,0:T(8,128)(2,1)S(1)} %get-tuple-element.7.returned), custom_call_target="tpu_custom_call" | custom-call | tf_op jit(solution)/shard_map/place_results/pallas_call | solution.py:362

commit v6 on v5

--- a/solution.py
+++ b/solution.py
@@ -62,7 +62,8 @@
 
 
 def targets(sign):
-    place, _ = position()
+    place, core = position()
+    sign = sign * (1 - 2 * core)
     steps = []
     for scale in (SIDE * SIDE, SIDE, 1):
         here = place // scale % SIDE
@@ -131,12 +132,12 @@
 
 
 def mixer_of(gram, low, mixer, j):
-    for i in range(j, STRIPS):
-        square = product(low[strip(i), :], low[:, strip(j)], ((1,), (0,)))
-        value = cubic_term * gram[strip(i), strip(j)] + quintic_term * square
-        mixer[strip(i), strip(j)] = value.astype(jnp.bfloat16)
-        if i != j:
-            mixer[strip(j), strip(i)] = value.T.astype(jnp.bfloat16)
+    column = slice(j * TILE, ROWS)
+    square = product(low[column, :], low[:, strip(j)], ((1,), (0,)))
+    value = cubic_term * gram[column, strip(j)] + quintic_term * square
+    mixer[column, strip(j)] = value.astype(jnp.bfloat16)
+    for i in range(j + 1, STRIPS):
+        mixer[strip(j), strip(i)] = value[strip(i - j), :].T.astype(jnp.bfloat16)
 
 
 def kernel(

time: 75.3 us -> 75.8 us (level)
  no operation moved by 1% of the time
where the time goes in v6:
time: 75.8 us; the launch traced here: 75.7 us
  Pallas kernels  74.9 us (99%)
  between operations  0.8 us (1%)
    pallas_call x1, Pallas kernels, on_device(): pl.pallas_call(kernel, out_shape=(pltpu.VMEM(shape, jnp.float32), blocks)...  72.3 us
    pallas_call x1, Pallas kernels, on_device(): pl.pallas_call(place_results, out_shape=(jax.ShapeDtypeStruct(shape, jnp....  2.58 us

profile of v6, /device:TPU:1, one launch (start us, length us, event | category | flops | bytes accessed | tf_op | source)
XLA Modules:
  0.0 75.7 jit_solution(11074703261574511023)
XLA Ops:
  0.6 72.3 %muon.1 = (f32[6,64,2560]{2,1,0:T(8,128)S(1)}, bf16[64,8,1920]{2,1,0:T(8,128)(2,1)S(1)}) custom-call(f32[6,64,2560]{2,1,0:T(8,128)} %bitcast.4, bf16[6,64,2560]{2,1,0:T(8,128)(2,1)} %bitcast.5, s32[64]{0:T(128)} %assignment.1), custom_call_target="tpu_custom_call" | custom-call | tf_op jit(solution)/shard_map/muon/pallas_call | solution.py:328
  73.0 2.6 %place_results.1 = (f32[6,64,2560]{2,1,0:T(8,128)}, bf16[6,64,2560]{2,1,0:T(8,128)(2,1)}) custom-call(f32[6,64,2560]{2,1,0:T(8,128)S(1)} %get-tuple-element.6.fresh, bf16[64,8,1920]{2,1,0:T(8,128)(2,1)S(1)} %get-tuple-element.7.returned), custom_call_target="tpu_custom_call" | custom-call | tf_op jit(solution)/shard_map/place_results/pallas_call | solution.py:363

commit v7 on v6

--- a/solution.py
+++ b/solution.py
@@ -62,8 +62,7 @@
 
 
 def targets(sign):
-    place, core = position()
-    sign = sign * (1 - 2 * core)
+    place, _ = position()
     steps = []
     for scale in (SIDE * SIDE, SIDE, 1):
         here = place // scale % SIDE
@@ -142,8 +141,8 @@
 
 def kernel(
     momentum, gradient, assignment, momentum_new, returned,
-    mom_in, grad_in, sent, arrived, relayed, x_now, x_next, gram, low, mixer, lines, squares,
-    load_sems, out_sem, in_sems, back_out_sem, back_sem, pair_out_sem, pair_sems,
+    mom_in, grad_in, sent, arrived, relayed, x_now, x_next, gram, low, mixer, lines, squares, owners,
+    plane_sem, owner_sem, load_sems, out_sem, in_sems, back_out_sem, back_sem, pair_out_sem, pair_sems,
 ):
     place, core = position()
     pair = (place, 1 - core)
@@ -158,12 +157,16 @@
     for group in range(GROUPS):
         for copy in load(group):
             copy.start()
+    fetch = pltpu.make_async_copy(assignment, owners, owner_sem)
+    fetch.start()
 
     barrier = pltpu.get_barrier_semaphore()
     pl.semaphore_signal(barrier, inc=1, device_id=pair, device_id_type=MESH)
 
     ahead = targets(1)
-    for target in ahead[1:]:
+    plane = [target for target, offset in zip(ahead, OFFSETS) if offset[2] == 0][1:]
+    line = [target for target, offset in zip(ahead, OFFSETS) if offset[:2] == (0, 0)][1:]
+    for target in plane + line:
         pl.semaphore_signal(barrier, inc=1, device_id=(target, core), device_id_type=MESH)
 
     def prepare(group, carry):
@@ -183,9 +186,12 @@
             pack_eight(lines.at[eight], sent, group * GROUP + eight * 8)
         return carry
 
-    lax.fori_loop(0, GROUPS, prepare, 0)
-
-    pl.semaphore_wait(barrier, CHIPS)
+    lax.fori_loop(0, GROUPS // 2, prepare, 0)
+    pl.semaphore_wait(barrier, 1 + len(plane) + len(line))
+    for target in line:
+        pl.semaphore_signal(plane_sem, inc=1, device_id=(target, core), device_id_type=MESH)
+    lax.fori_loop(GROUPS // 2, GROUPS, prepare, 0)
+    pl.semaphore_wait(plane_sem, len(line))
 
     pltpu.make_async_copy(sent.at[place], arrived.at[0], in_sems.at[0]).start()
 
@@ -251,7 +257,8 @@
         for j in range(i + 1):
             keep_block(gram, low, i, j, gram_block(x_next, i, j))
 
-    active = assignment[place] >= 0
+    fetch.wait()
+    active = owners[place] >= 0
     made = set()
 
     def finish(first, last):
@@ -331,7 +338,7 @@
         in_specs=[
             pl.BlockSpec(memory_space=pl.ANY),
             pl.BlockSpec(memory_space=pl.ANY),
-            pl.BlockSpec(memory_space=pltpu.SMEM),
+            pl.BlockSpec(memory_space=pl.ANY),
         ],
         out_specs=[pl.BlockSpec(memory_space=pltpu.VMEM)] * 2,
         scratch_shapes=[
@@ -347,6 +354,9 @@
             pltpu.VMEM((ROWS, ROWS), jnp.bfloat16),
             line_space,
             pltpu.VMEM((8, LANES), jnp.float32),
+            pltpu.SMEM((CHIPS,), jnp.int32),
+            pltpu.SemaphoreType.REGULAR,
+            pltpu.SemaphoreType.DMA,
             pltpu.SemaphoreType.DMA((2, GROUPS)),
             pltpu.SemaphoreType.DMA,
             pltpu.SemaphoreType.DMA((PIECES,)),

time: 75.8 us -> 75.6 us (level)
  no operation moved by 1% of the time
where the time goes in v7:
time: 75.6 us; the launch traced here: 75.5 us
  Pallas kernels  74.7 us (99%)
  between operations  0.8 us (1%)
    pallas_call x1, Pallas kernels, on_device(): pl.pallas_call(kernel, out_shape=(pltpu.VMEM(shape, jnp.float32), blocks)...  72.1 us
    pallas_call x1, Pallas kernels, on_device(): pl.pallas_call(place_results, out_shape=(jax.ShapeDtypeStruct(shape, jnp....  2.58 us

profile of v7, /device:TPU:1, one launch (start us, length us, event | category | flops | bytes accessed | tf_op | source)
XLA Modules:
  0.0 75.5 jit_solution(17116320080654989020)
XLA Ops:
  0.6 72.1 %muon.1 = (f32[6,64,2560]{2,1,0:T(8,128)S(1)}, bf16[64,8,1920]{2,1,0:T(8,128)(2,1)S(1)}) custom-call(f32[6,64,2560]{2,1,0:T(8,128)} %bitcast.4, bf16[6,64,2560]{2,1,0:T(8,128)(2,1)} %bitcast.5, s32[64]{0:T(128)} %assignment.1), custom_call_target="tpu_custom_call" | custom-call | tf_op jit(solution)/shard_map/muon/pallas_call | solution.py:335
  72.7 2.6 %place_results.1 = (f32[6,64,2560]{2,1,0:T(8,128)}, bf16[6,64,2560]{2,1,0:T(8,128)(2,1)}) custom-call(f32[6,64,2560]{2,1,0:T(8,128)S(1)} %get-tuple-element.6.fresh, bf16[64,8,1920]{2,1,0:T(8,128)(2,1)S(1)} %get-tuple-element.7.returned), custom_call_target="tpu_custom_call" | custom-call | tf_op jit(solution)/shard_map/place_results/pallas_call | solution.py:373

commit v8 on v7

--- a/solution.py
+++ b/solution.py
@@ -31,7 +31,7 @@
 GROUPS = CHIPS // GROUP
 PIECE = 4
 PIECES = CHIPS // PIECE
-SHARES = ((0, 1), (1, GROUPS))
+SHARES = tuple((group, group + 1) for group in range(GROUPS))
 TILE = 256
 STRIPS = ROWS // TILE
 
@@ -309,9 +309,11 @@
 
 
 def place_results(fresh, returned, momentum_new, update, rows_out, lines, fresh_sem, group_sems):
-    whole = pltpu.make_async_copy(fresh, momentum_new, fresh_sem)
-    whole.start()
-    copies = []
+    copies = [
+        pltpu.make_async_copy(fresh.at[row], momentum_new.at[row], fresh_sem.at[row]) for row in range(LOCAL)
+    ]
+    for copy in copies:
+        copy.start()
     for group in range(GROUPS):
         rows = pl.ds(group * GROUP, GROUP)
 
@@ -325,7 +327,6 @@
         copies[-1].start()
     for copy in copies:
         copy.wait()
-    whole.wait()
 
 
 def on_device(momentum, gradient, assignment):
@@ -378,7 +379,7 @@
         scratch_shapes=[
             pltpu.VMEM(shape, jnp.bfloat16),
             line_space,
-            pltpu.SemaphoreType.DMA,
+            pltpu.SemaphoreType.DMA((LOCAL,)),
             pltpu.SemaphoreType.DMA((GROUPS,)),
         ],
         compiler_params=pltpu.CompilerParams(vmem_limit_bytes=32 * 2**20),

time: 75.6 us -> 75.8 us (level)
  no operation moved by 1% of the time
where the time goes in v8:
time: 75.8 us; the launch traced here: 75.7 us
  Pallas kernels  74.9 us (99%)
  between operations  0.8 us (1%)
    pallas_call x1, Pallas kernels, on_device(): pl.pallas_call(kernel, out_shape=(pltpu.VMEM(shape, jnp.float32), blocks)...  72.3 us
    pallas_call x1, Pallas kernels, on_device(): pl.pallas_call(place_results, out_shape=(jax.ShapeDtypeStruct(shape, jnp....  2.62 us

profile of v8, /device:TPU:1, one launch (start us, length us, event | category | flops | bytes accessed | tf_op | source)
XLA Modules:
  0.0 75.7 jit_solution(16204125253380136529)
XLA Ops:
  0.6 72.3 %muon.1 = (f32[6,64,2560]{2,1,0:T(8,128)S(1)}, bf16[64,8,1920]{2,1,0:T(8,128)(2,1)S(1)}) custom-call(f32[6,64,2560]{2,1,0:T(8,128)} %bitcast.4, bf16[6,64,2560]{2,1,0:T(8,128)(2,1)} %bitcast.5, s32[64]{0:T(128)} %assignment.1), custom_call_target="tpu_custom_call" | custom-call | tf_op jit(solution)/shard_map/muon/pallas_call | solution.py:336
  72.9 2.6 %place_results.1 = (f32[6,64,2560]{2,1,0:T(8,128)}, bf16[6,64,2560]{2,1,0:T(8,128)(2,1)}) custom-call(f32[6,64,2560]{2,1,0:T(8,128)S(1)} %get-tuple-element.6.fresh, bf16[64,8,1920]{2,1,0:T(8,128)(2,1)S(1)} %get-tuple-element.7.returned), custom_call_target="tpu_custom_call" | custom-call | tf_op jit(solution)/shard_map/place_results/pallas_call | solution.py:374

commit v9 on v8

--- a/solution.py
+++ b/solution.py
@@ -40,6 +40,10 @@
     return lax.axis_index("dp"), lax.axis_index("tensor")
 
 
+def hops_of(offset):
+    return sum(min(step, SIDE - step) for step in offset)
+
+
 def spread_offsets():
     sets = []
     for offset in ((x, y, z) for x in range(SIDE) for y in range(SIDE) for z in range(SIDE)):
@@ -47,7 +51,7 @@
         alike = dict.fromkeys(tuple(sign * step % SIDE for step in turn) for sign in (1, -1) for turn in turns)
         if offset == min(alike):
             sets.append(list(alike))
-    hops = [sum(min(step, SIDE - step) for step in alike[0]) for alike in sets]
+    hops = [hops_of(alike[0]) for alike in sets]
     ranked, rest = [], {}
     for index in range(1, len(sets)):
         rest.setdefault(hops[index], []).append(index)
@@ -294,7 +298,7 @@
     behind = targets(-1)
     for first, last in SHARES:
         finish(first, last)
-        for slot in range(first * GROUP, last * GROUP):
+        for slot in sorted(range(first * GROUP, last * GROUP), key=lambda slot: -hops_of(OFFSETS[slot])):
             if slot == 0:
                 pltpu.make_async_copy(sent.at[0], returned.at[place], back_sem).start()
             else:
@@ -332,7 +336,7 @@
 def on_device(momentum, gradient, assignment):
     shape = (LOCAL, CHIPS, WIDTH)
     blocks = pltpu.VMEM((CHIPS, *BLOCK), jnp.bfloat16)
-    line_space = pltpu.VMEM((2 * GROUPS, 8 * PITCH, LANES), jnp.float32)
+    line_space = pltpu.VMEM((2 * GROUPS, 9 * PITCH, LANES), jnp.float32)
     fresh, returned = pl.pallas_call(
         kernel,
         out_shape=(pltpu.VMEM(shape, jnp.float32), blocks),

time: 75.8 us -> 75.2 us (level)
  no operation moved by 1% of the time
where the time goes in v9:
time: 75.2 us; the launch traced here: 75 us
  Pallas kernels  74.2 us (99%)
  between operations  0.8 us (1%)
    pallas_call x1, Pallas kernels, on_device(): pl.pallas_call(kernel, out_shape=(pltpu.VMEM(shape, jnp.float32), blocks)...  71.6 us
    pallas_call x1, Pallas kernels, on_device(): pl.pallas_call(place_results, out_shape=(jax.ShapeDtypeStruct(shape, jnp....  2.62 us

profile of v9, /device:TPU:1, one launch (start us, length us, event | category | flops | bytes accessed | tf_op | source)
XLA Modules:
  0.0 75.0 jit_solution(2387734881449509723)
XLA Ops:
  0.6 71.6 %muon.1 = (f32[6,64,2560]{2,1,0:T(8,128)S(1)}, bf16[64,8,1920]{2,1,0:T(8,128)(2,1)S(1)}) custom-call(f32[6,64,2560]{2,1,0:T(8,128)} %bitcast.4, bf16[6,64,2560]{2,1,0:T(8,128)(2,1)} %bitcast.5, s32[64]{0:T(128)} %assignment.1), custom_call_target="tpu_custom_call" | custom-call | tf_op jit(solution)/shard_map/muon/pallas_call | solution.py:340
  72.3 2.6 %place_results.1 = (f32[6,64,2560]{2,1,0:T(8,128)}, bf16[6,64,2560]{2,1,0:T(8,128)(2,1)}) custom-call(f32[6,64,2560]{2,1,0:T(8,128)S(1)} %get-tuple-element.6.fresh, bf16[64,8,1920]{2,1,0:T(8,128)(2,1)S(1)} %get-tuple-element.7.returned), custom_call_target="tpu_custom_call" | custom-call | tf_op jit(solution)/shard_map/place_results/pallas_call | solution.py:378
